TPU v7x, 512 devices: a whole 4x4x16 slice. The times are simulated.
512 devices in a mesh: dp: 64 (over z_lo, x, y), fsdp: 8 (over z_hi, core).
Axes of the slice: x: 4, y: 4, z: 16 (z_hi: 4, z_lo: 4; z = z_hi * 4 + z_lo), core: 2. Of those that a mesh axis runs over, the one named last changes fastest.
Arguments:
- frames: bfloat16 [65536, 1536], P(('dp', 'fsdp')), may hold values from -6 to 6
- frame_mask: int32 [65536], P(('dp', 'fsdp')), may hold values 0 or 1
- block_dest: int32 [16384], P(('dp', 'fsdp')), may hold values from 0 to 63, as said below
- codes_first: int32 [1536, 24], P(None, 'fsdp'), may hold values from 0 to 255
- codes_second: int32 [1536, 24], P(None, 'fsdp'), may hold values from 0 to 255
- codebook_first: float32 [256, 128], replicated, may hold values from -0.15309311 to 0.15309311
- codebook_second: float32 [256, 128], replicated, may hold values from -0.07654656 to 0.07654656
- rotation: bfloat16 [1536, 1536], P('fsdp'), may hold values from -0.15625 to 0.15625
- gain: float32 [1536], replicated, may hold values from 0.25 to 1.75
- scale: float32 [3072], replicated, may hold values from 0.5 to 2
- cotangent: bfloat16 [65536, 3072], P(('dp', 'fsdp')), may hold values from -24 to 24
Outputs:
- activation: bfloat16 [65536, 3072], P(('dp', 'fsdp'))
- moved_frame_gradient: bfloat16 [65536, 1536], P(('dp', 'fsdp'))
- scale_grad: float32 [3072], P('fsdp')
- gain_grad: float32 [1536], replicated
Inputs may be any that keep to these rules, and one draw needn't show every extreme that they name: `block_dest`: for every fsdp index and slot, the blocks of that slot on the 64 dp indices go to 64 different dp indices; the 32 blocks of one device go to different dp indices.
All inputs are finite; a program needn't handle non-finite values. No bound on the sum of `frame_mask` on one device may be relied on, other than what follows from the above.
Results may differ from a plain program's by a relative error of at most 0.0076.
Values may be sent and summed in bfloat16 or wider, within the bound.
A program may use at most 128 MiB of HBM per device.

v0:
```python
import jax
import jax.numpy as jnp
from jax import lax
from jax.sharding import PartitionSpec as P


def dequantize(first_codes, second_codes, codebook_first, codebook_second):
    looked = jnp.take(codebook_first, first_codes, axis=0) + jnp.take(
        codebook_second, second_codes, axis=0
    )
    return looked.reshape(
        first_codes.shape[0], first_codes.shape[1] * codebook_first.shape[1]
    ).astype(jnp.bfloat16)


def body(
    frames,
    frame_mask,
    block_dest,
    codes_first,
    codes_second,
    codebook_first,
    codebook_second,
    rotation,
    gain,
    scale,
    cotangent,
):
    dp_count = lax.axis_size("dp")
    rows, width = frames.shape
    blocks = block_dest.shape[0]
    blk_rows = rows // blocks
    slot_ids = jnp.arange(blocks, dtype=jnp.int32)
    target_ids = jnp.arange(dp_count, dtype=jnp.int32)
    chosen = block_dest[None, :] == target_ids[:, None]
    pick = chosen.astype(jnp.bfloat16)
    outgoing = jnp.dot(
        pick, frames.reshape(blocks, blk_rows * width), preferred_element_type=jnp.float32
    ).astype(jnp.bfloat16)
    mask_out = jnp.dot(
        pick,
        frame_mask.reshape(blocks, blk_rows).astype(jnp.bfloat16),
        preferred_element_type=jnp.float32,
    )
    slot_out = jnp.sum(jnp.where(chosen, slot_ids[None, :], 0), axis=1).astype(jnp.float32)
    valid_out = jnp.any(chosen, axis=1).astype(jnp.float32)
    meta = jnp.concatenate([mask_out, slot_out[:, None], valid_out[:, None]], axis=1).astype(
        jnp.bfloat16
    )
    incoming, info = (
        lax.all_to_all(outgoing, "dp", split_axis=0, concat_axis=0, tiled=True),
        lax.all_to_all(meta, "dp", split_axis=0, concat_axis=0, tiled=True),
    )
    place = (
        info[:, blk_rows][None, :].astype(jnp.float32) == slot_ids[:, None].astype(jnp.float32)
    ) & (info[:, blk_rows + 1][None, :] > 0.5)
    place = place.astype(jnp.bfloat16)
    moved = (
        jnp.dot(place, incoming, preferred_element_type=jnp.float32)
        .astype(jnp.bfloat16)
        .reshape(rows, width)
    )
    live = jnp.dot(place, info[:, :blk_rows], preferred_element_type=jnp.float32).reshape(rows, 1)
    segment = dequantize(codes_first, codes_second, codebook_first, codebook_second)
    whole_rotation = lax.all_gather(rotation, "fsdp", axis=0, tiled=True)
    local = jnp.dot(whole_rotation, segment, preferred_element_type=jnp.float32).astype(
        jnp.bfloat16
    )
    weight = lax.all_gather(local, "fsdp", axis=1, tiled=True)
    xval = moved.astype(jnp.float32)
    centered_input = xval - jnp.mean(xval, axis=1, keepdims=True)
    inverse_deviation = lax.rsqrt(
        jnp.mean(centered_input * centered_input, axis=1, keepdims=True) + 1e-06
    )
    standardized_input = centered_input * inverse_deviation
    normalized_output = (standardized_input * gain).astype(jnp.bfloat16)
    inner = jnp.dot(normalized_output, weight, preferred_element_type=jnp.float32)
    pre = inner * scale
    sig = jax.nn.sigmoid(pre)
    activation = (pre * sig * live).astype(jnp.bfloat16)
    dpre = cotangent.astype(jnp.float32) * live * sig * (1.0 + pre * (1.0 - sig))
    scale_part = jnp.sum(dpre * inner, axis=0)
    dinner = (dpre * scale).astype(jnp.bfloat16)
    normalized_gradient = lax.dot_general(
        dinner, weight, (((1,), (1,)), ((), ())), preferred_element_type=jnp.float32
    )
    partial_gain_gradient = jnp.sum(normalized_gradient * standardized_input, axis=0)
    standardized_gradient = normalized_gradient * gain
    moved_frame_gradient = inverse_deviation * (
        standardized_gradient
        - jnp.mean(standardized_gradient, axis=1, keepdims=True)
        - standardized_input
        * jnp.mean(standardized_gradient * standardized_input, axis=1, keepdims=True)
    )
    scale_shard = lax.psum_scatter(scale_part, "fsdp", scatter_dimension=0, tiled=True)
    scale_grad = lax.psum(scale_shard, "dp")
    gain_grad = lax.psum(partial_gain_gradient, ("dp", "fsdp"))
    return (activation, moved_frame_gradient.astype(jnp.bfloat16), scale_grad, gain_grad)


def solution(mesh):
    placed = (
        P(("dp", "fsdp"), None),
        P(("dp", "fsdp")),
        P(("dp", "fsdp")),
        P(None, "fsdp"),
        P(None, "fsdp"),
        P(),
        P(),
        P("fsdp", None),
        P(),
        P(),
        P(("dp", "fsdp"), None),
    )
    return jax.shard_map(
        body,
        mesh=mesh,
        in_specs=placed,
        out_specs=(P(("dp", "fsdp"), None), P(("dp", "fsdp"), None), P("fsdp"), P()),
        check_vma=False,
    )
```

profile of v0, /device:TPU:8, one launch (start us, length us, event | category | flops | bytes accessed | tf_op | source)
XLA Modules:
  0.0 657.4 jit_solution(7083729380413976480)
XLA Ops:
  7.2 0.7 all-gather.3.cloned.1.call-update
  8.0 0.7 compare_select_fusion.1
  9.0 0.5 reshape.163
  9.5 7.3 %gather_fusion = f32[4608,128]{1,0:T(8,128)S(1)} fusion(f32[256,128]{1,0:T(8,128)S(1)} %copy-done, s32[5120]{0:T(1024)S(1)} %pad_clamp_fusion.1), kind=kCustom, calls=%fused_computation.clone | custom fusion | bytes 4737024 | tf_op jit(solution)/shard_map/jit(_take)/gather | solution.py:8
  16.8 2.7 reshape.166
  19.8 0.5 reshape.167
  20.4 7.2 %gather_fusion.1 = f32[4608,128]{1,0:T(8,128)S(1)} fusion(f32[256,128]{1,0:T(8,128)S(1)} %copy-done.1, s32[5120]{0:T(1024)S(1)} %pad_clamp_fusion), kind=kCustom, calls=%fused_computation.1.clone | custom fusion | bytes 4737024 | tf_op jit(solution)/shard_map/jit(_take)/gather | solution.py:8
  27.6 2.6 reshape.170
  30.3 0.4 copy.44
  31.1 5.8 fusion.2
  36.8 0.9 copy.48
  37.7 80.9 %all-gather.3.cloned.1.call-done = bf16[1536,1536]{1,0:T(8,128)(2,1)} async-done(((bf16[192,1536]{1,0:T(8,128)(2,1)}), bf16[1536,1536]{1,0:T(8,128)(2,1)}) %all-gather.3.cloned.1.call-update) | async-done | bytes 4718608 | tf_op jit(solution)/shard_map/all_gather | solution.py:65
  118.6 5.4 fusion.3
  124.6 0.7 copy.41
  125.3 7.8 %all-to-all-start = ((bf16[64,1,6]{2,1,0:T(2,128)(2,1)}), bf16[64,1,6]{2,1,0:T(2,128)(2,1)S(1)}, u32[]{:S(2)}, u32[]{:S(2)}) async-start(bf16[64,1,6]{2,1,0:T(2,128)(2,1)} %copy.41), calls=%async_computation | async-start | bytes 65536 | tf_op jit(solution)/shard_map/all_to_all | solution.py:52
  133.4 0.5 fusion
  133.9 0.5 broadcast.71
  134.4 1.2 reduce
  135.6 1.5 reshape.172
  137.0 5.1 all-to-all-done
  142.2 5.6 all-to-all-start.1
  147.8 1.3 dynamic-slice
  150.1 115.1 %all-to-all-done.1 = bf16[64,2,3072]{2,1,0:T(2,128)(2,1)S(1)} async-done(((bf16[64,2,3072]{2,1,0:T(2,128)(2,1)}), bf16[64,2,3072]{2,1,0:T(2,128)(2,1)S(1)}, u32[]{:S(2)}, u32[]{:S(2)}) %all-to-all-start.1) | async-done | bytes 786464 | tf_op jit(solution)/shard_map/all_to_all | solution.py:51
  265.3 0.6 reshape.173
  265.9 0.6 fusion.1
  267.2 0.5 copy-done.8
  267.7 8.2 %multiply_reduce_fusion = (f32[3072]{0:T(1024)S(1)}, bf16[128,3072]{1,0:T(8,128)(2,1)}, f32[128,3072]{1,0:T(8,128)S(1)}) fusion(f32[3072]{0:T(1024)S(1)} %copy-done.9, f32[128]{0:T(128)S(1)} %mul.98, bf16[128,3072]{1,0:T(8,128)(2,1)S(1)} %copy-done.8, bf16[1536,3072]{0,1:T(8,128)(2,1)} %all-gather.5.cloned.1.call-done, f32[128,1536]{1,0:T(8,128)S(1)} %reshape.141, ...), kind=kOutput, calls=%fused_computation.10 | convolution fusion | flops 1215034368 | bytes 13401600 | tf_op jit(solution)/shard_map/dot_general | solution.py:77
  275.9 2.0 multiply_reduce_fusion.1
  277.9 150.8 %psum.15 = f32[1536]{0:T(1024)} all-reduce(f32[1536]{0:T(1024)S(1)} %get-tuple-element.5), channel_id=1, replica_groups=mesh['dp'=64,'fsdp'=8] {'dp','fsdp'}, use_global_device_ids=true, to_apply=%region_10.12 | all-reduce | flops 1536 | bytes 12288 | tf_op jit(solution)/shard_map/psum | solution.py:97
  428.7 37.0 %all-reduce = f32[3072]{0:T(1024)S(1)} all-reduce(f32[3072]{0:T(1024)S(1)} %get-tuple-element.8), channel_id=2, replica_groups=mesh['dp'=64,'fsdp'=8] {'fsdp'}, use_global_device_ids=true, to_apply=%region_7.9.clone | all-reduce | flops 3072 | bytes 24576
  465.8 183.7 %psum.14 = f32[384]{0:T(512)} all-reduce(f32[384]{0:T(512)S(1)} %dynamic-slice.1), channel_id=1, replica_groups=mesh['dp'=64,'fsdp'=8] {'dp'}, use_global_device_ids=true, to_apply=%region_8.10 | all-reduce | flops 384 | bytes 3072 | tf_op jit(solution)/shard_map/psum | solution.py:96
  649.5 1.1 multiply_convert_fusion.3
  (55 shorter events, 3.2 us)
Async XLA Ops:
  7.2 2.3 copy-start
  7.2 111.4 %all-gather.3.cloned.1.call-start = ((), (), s32[]{:S(2)}) async-start(), calls=%async_computation.2 | async-start | bytes 5308416 | tf_op jit(solution)/shard_map/all_gather | solution.py:65
  7.9 259.3 %all-gather.5.cloned.1.call-start = ((), (), s32[]{:S(2)}) async-start(), calls=%async_computation.3 | async-start | bytes 10616832 | tf_op jit(solution)/shard_map/all_gather | solution.py:69
  16.8 2.7 copy-start.4
  19.5 0.9 copy-start.1
  27.6 2.6 copy-start.3
  118.6 5.4 copy-start.10
  118.6 5.5 copy-start.6
  124.0 9.1 %copy-start.2 = (bf16[128,1536]{1,0:T(8,128)(2,1)S(1)}, bf16[128,1536]{1,0:T(8,128)(2,1)}, u32[]{:S(2)}) copy-start(bf16[128,1536]{1,0:T(8,128)(2,1)} %param.13) | copy-start | bytes 1179652
  125.3 16.8 %all-to-all-start = ((bf16[64,1,6]{2,1,0:T(2,128)(2,1)}), bf16[64,1,6]{2,1,0:T(2,128)(2,1)S(1)}, u32[]{:S(2)}, u32[]{:S(2)}) async-start(bf16[64,1,6]{2,1,0:T(2,128)(2,1)} %copy.41), calls=%async_computation | async-start | bytes 65536 | tf_op jit(solution)/shard_map/all_to_all | solution.py:52
  142.2 123.1 %all-to-all-start.1 = ((bf16[64,2,3072]{2,1,0:T(2,128)(2,1)}), bf16[64,2,3072]{2,1,0:T(2,128)(2,1)S(1)}, u32[]{:S(2)}, u32[]{:S(2)}) async-start(bf16[64,2,3072]{2,1,0:T(2,128)(2,1)} %reshape.172), calls=%async_computation.1 | async-start | bytes 1572864 | tf_op jit(solution)/shard_map/all_to_all | solution.py:51
  266.5 0.7 copy-start.5
  266.5 1.1 copy-start.8
  266.5 1.1 copy-start.9
  267.7 8.2 %copy-start.7 = (bf16[1536,3072]{0,1:T(8,128)(2,1)S(1)}, bf16[1536,3072]{0,1:T(8,128)(2,1)}, u32[]{:S(2)}) copy-start(bf16[1536,3072]{0,1:T(8,128)(2,1)} %all-gather.5.cloned.1.call-done) | copy-start | bytes 28311556
Sparse Core Ops, SparseCore 0:
  10.1 108.4 all-gather.2
  124.2 137.5 all-gather.4
where the time goes:
time: 658 us; the launch traced here: 657 us
  blocking collectives  372 us (57%)
  waiting for transfers between devices  202 us (31%)
  local copies, waits for them, and re-layouts  29 us (4%)
  matrix products  17.1 us (3%)
  between operations  15 us (2%)
  starting transfers between devices  13.4 us (2%)
  other arithmetic  9.41 us (1%)
    psum x1, blocking collectives, body(): scale_grad = lax.psum(scale_shard, 'dp')  184 us
    psum x1, blocking collectives, body(): gain_grad = lax.psum(partial_gain_gradient, ('dp', 'fsdp'))  151 us
    all_to_all x1, waiting for transfers between devices, body(): lax.all_to_all(outgoing, 'dp', split_axis=0, concat_axis=0, tiled=True)  115 us
    all_gather x1, waiting for transfers between devices, body(): whole_rotation = lax.all_gather(rotation, 'fsdp', axis=0, tiled=True)  80.9 us
    unnamed x1, blocking collectives  37 us
  transfers between devices with their start and end apart: 4, of which 3 were waited for; matrix products, arithmetic and copies ran while one was open for 6% of the time, Pallas kernels for 0%

commit v1 on v0

v1 whole, which is shorter than its diff:
```python
import functools

import jax
import jax.numpy as jnp
from jax import lax
from jax.experimental import pallas as pl
from jax.experimental.pallas import tpu as pltpu
from jax.sharding import PartitionSpec as P

MESH = pl.DeviceIdType.MESH
F32 = jnp.float32
BF16 = jnp.bfloat16
NDP, NF = 64, 8
ROWS, D, FF = 128, 1536, 3072
SEG = 384
MSG = 16
PR, PC = 48, 384


def iota(shape, dim, dtype=jnp.int32):
    found = lax.broadcasted_iota(jnp.int32, shape, dim)
    return found if dtype == jnp.int32 else found.astype(dtype)


def kernel(
    frames, drow, mrow, cpk, cb1, cb2, rot, gain, scale, cot,
    act, mfg, red,
    outb, inb, wout, win, codes, turned, cbcat, rfull, deq, xhat, normed, ubuf, dinner, vbuf, dnorm,
    sbuf, gbuf, msg_a, got_a, msg_b, got_b, msg_c, got_c,
    s_frames, r_frames, s_meta, r_meta, s_own, s_code, r_code, s_codex, r_codex,
    s_r0, r_r0, s_r1, r_r1, s_r2, r_r2, s_rx, r_rx, s_red, r_red,
):
    dp = lax.axis_index("dp")
    fs = lax.axis_index("fsdp")
    zlo, xy = dp // 16, dp % 16
    xx, yy = xy // 4, xy % 4
    zhi, core = fs // 2, fs % 2
    other = zhi * 2 + 1 - core

    def to(src, dst, send, recv, d, f):
        return pltpu.make_async_remote_copy(
            src_ref=src, dst_ref=dst, send_sem=send, recv_sem=recv,
            device_id=(d, f), device_id_type=MESH,
        )

    def wait_for(ref, sem):
        pltpu.make_async_copy(ref, ref, sem).wait()

    barrier = pltpu.get_barrier_semaphore()

    def hello_dp(j, _):
        pl.semaphore_signal(barrier, inc=1, device_id=((dp + j) % NDP, fs), device_id_type=MESH)
        return 0

    def hello_fs(j, _):
        pl.semaphore_signal(barrier, inc=1, device_id=(dp, (fs + j) % NF), device_id_type=MESH)
        return 0

    lax.fori_loop(1, NDP, hello_dp, 0)
    lax.fori_loop(1, NF, hello_fs, 0)

    lane = iota((1, ROWS), 1)
    dest = drow[...]
    key = jnp.concatenate([dest * MSG + s * 4 + lane % 4 for s in range(4)], axis=1)
    wide = jnp.concatenate([frames[:, s * SEG : (s + 1) * SEG] for s in range(4)], axis=0)

    def fill(k, _):
        row = iota((256, 4 * ROWS), 0) + k * 256
        pick = jnp.where(row == key, 1.0, 0.0).astype(BF16)
        outb[pl.ds(pl.multiple_of(k * 256, 256), 256), :] = jnp.dot(
            pick, wide, preferred_element_type=F32
        ).astype(BF16)
        return 0

    lax.fori_loop(0, 4, fill, 0)
    wout[...] = jnp.where(iota((NDP, 1, ROWS), 0) == dest[None], 1.0 + mrow[...][None], 0.0)

    for k, book in enumerate((cb1, cb2)):
        value = book[...]
        high = value.astype(BF16)
        cbcat[k * 256 : (k + 1) * 256, 0:128] = high
        cbcat[k * 256 : (k + 1) * 256, 128:256] = (value - high.astype(F32)).astype(BF16)
    codes[fs] = cpk[...]
    rfull[pl.ds(pl.multiple_of(fs * 192, 192), 192), :] = rot[...]
    win[dp] = wout[dp]

    pl.semaphore_wait(barrier, NDP - 1 + NF - 1)

    def rows_of(f):
        return pl.ds(pl.multiple_of(f * 192, 192), 192)

    def piece(f, i, j):
        return rfull.at[
            pl.ds(pl.multiple_of(f * 192 + i * PR, 16), PR), pl.ds(pl.multiple_of(j * PC, 128), PC)
        ]

    def away(k):
        return ((zhi + k) % 4) * 2 + core

    def back(k):
        return ((zhi + 4 - k) % 4) * 2 + core

    for k in (1, 2, 3):
        to(cpk, codes.at[fs], s_code.at[k - 1], r_code.at[k - 1], dp, away(k)).start()
    to(cpk, codes.at[fs], s_codex.at[0], r_codex.at[0], dp, other).start()
    for k in (1, 2, 3):
        to(piece(fs, xx, yy), piece(fs, xx, yy), s_r0.at[k - 1], r_r0.at[k - 1], dp, away(k)).start()
    to(rfull.at[rows_of(fs), :], rfull.at[rows_of(fs), :], s_rx.at[0], r_rx.at[0], dp, other).start()

    def block(c):
        return pl.ds(pl.multiple_of(c * MSG, MSG), MSG)

    def send_block(j, _):
        peer = (dp + j) % NDP
        to(wout.at[peer], win.at[dp], s_meta, r_meta, peer, fs).start()
        to(outb.at[block(peer), :], inb.at[block(dp), :], s_frames, r_frames, peer, fs).start()
        return 0

    lax.fori_loop(1, NDP, send_block, 0)
    own = pltpu.make_async_copy(outb.at[block(dp), :], inb.at[block(dp), :], s_own)
    own.start()

    def look_up(f):
        part = jnp.concatenate([codes[f].astype(F32), jnp.zeros((32, 128), F32)], axis=0)
        turned[...] = part.T
        entry = iota((128, 256), 1, F32)

        def step(t, _):
            table = turned[...]
            hot = jnp.concatenate(
                [
                    jnp.concatenate(
                        [
                            jnp.where(table[:, h * 8 + b * 3 + q : h * 8 + b * 3 + q + 1] == entry, 1.0, 0.0).astype(BF16)
                            for b in range(2)
                        ],
                        axis=1,
                    )
                    for h in range(2)
                    for q in range(3)
                ],
                axis=0,
            )
            found = jnp.dot(hot, cbcat[...], preferred_element_type=F32)
            found = (found[:, :128] + found[:, 128:]).astype(BF16)
            for h in range(2):
                for q in range(3):
                    deq[
                        pl.ds(pl.multiple_of(t * 256 + h * 128, 128), 128),
                        pl.ds(pl.multiple_of(f * 384 + q * 128, 128), 128),
                    ] = found[(h * 3 + q) * 128 : (h * 3 + q + 1) * 128, :]
            turned[...] = pltpu.roll(table, 112, 1)
            return 0

        lax.fori_loop(0, 6, step, 0)

    look_up(fs)

    for k in (1, 2, 3):
        wait_for(codes.at[back(k)], r_code.at[k - 1])
        to(codes.at[back(k)], codes.at[back(k)], s_codex.at[k], r_codex.at[k], dp, other).start()
    for k in (1, 2, 3):
        wait_for(piece(back(k), xx, yy), r_r0.at[k - 1])
        for d in (1, 2, 3):
            nx = (xx + d * (1 - core)) % 4
            ny = (yy + d * core) % 4
            to(piece(back(k), xx, yy), piece(back(k), xx, yy), s_r1, r_r1.at[k - 1], zlo * 16 + nx * 4 + ny, fs).start()

    wait_for(codes.at[other], r_codex.at[0])
    look_up(other)
    look_up(back(1))

    for k in (1, 2, 3):
        wait_for(rfull.at[0:144, 0:PC], r_r1.at[k - 1])

        def spread(n, _):
            d, m = n // 4 + 1, n % 4
            nx = (xx + d * core) % 4
            ny = (yy + d * (1 - core)) % 4
            px = m * (1 - core) + xx * core
            py = yy * (1 - core) + m * core
            to(piece(back(k), px, py), piece(back(k), px, py), s_r2, r_r2.at[k - 1], zlo * 16 + nx * 4 + ny, fs).start()
            return 0

        lax.fori_loop(0, 12, spread, 0)

    look_up(back(2))
    look_up(back(3))
    for k in (1, 2, 3):
        wait_for(codes.at[back(k)], r_codex.at[k])

    def other_of(f):
        return f + 1 - 2 * core

    look_up(other_of(back(1)))

    for k in (1, 2, 3):
        wait_for(rfull.at[0:576, 0:PC], r_r2.at[k - 1])
        to(rfull.at[rows_of(back(k)), :], rfull.at[rows_of(back(k)), :], s_rx.at[k], r_rx.at[k], dp, other).start()

    look_up(other_of(back(2)))
    look_up(other_of(back(3)))

    wait_for(win.at[0 : NDP - 1], r_meta)
    wait_for(inb.at[0 : (NDP - 1) * MSG, :], r_frames)
    own.wait()
    meta = win[...]
    mask_row = jnp.sum(meta, axis=0) - 1.0
    src_row = jnp.sum(jnp.where(meta > 0.5, iota((NDP, 1, ROWS), 0, F32), 0.0), axis=0)
    eye = iota((ROWS, ROWS), 0) == iota((ROWS, ROWS), 1)
    live = jnp.sum(jnp.where(eye, mask_row, 0.0), axis=1, keepdims=True)
    src = jnp.sum(jnp.where(eye, src_row, 0.0), axis=1, keepdims=True)
    first = src * float(MSG) + (iota((ROWS, 1), 0) % 4).astype(F32)
    for s in range(4):
        put = jnp.where(iota((ROWS, NDP * MSG), 1, F32) == first + 4.0 * s, 1.0, 0.0).astype(BF16)
        xhat[:, s * SEG : (s + 1) * SEG] = jnp.dot(put, inb[...], preferred_element_type=F32)
    xval = xhat[...]
    centered = xval - jnp.sum(xval, axis=1, keepdims=True) * (1.0 / D)
    inv = lax.rsqrt(jnp.sum(centered * centered, axis=1, keepdims=True) * (1.0 / D) + 1e-06)
    standard = centered * inv
    xhat[...] = standard
    normed[...] = (standard * gain[...]).astype(BF16)

    for k in range(4):
        wait_for(rfull.at[rows_of(other_of(back(k))), :], r_rx.at[k])

    def forward_u(n, _):
        cols = pl.ds(pl.multiple_of(n * 512, 512), 512)
        ubuf[:, cols] = jnp.dot(normed[...], rfull[:, cols], preferred_element_type=F32).astype(BF16)
        return 0

    lax.fori_loop(0, 3, forward_u, 0)

    sbuf[...] = jnp.zeros_like(sbuf)
    gbuf[...] = jnp.zeros_like(gbuf)

    def forward(n, _):
        cols = pl.ds(pl.multiple_of(n * 768, 768), 768)
        inner = jnp.dot(ubuf[...], deq[:, cols], preferred_element_type=F32)
        sc = scale[:, cols]
        pre = inner * sc
        sig = 1.0 / (1.0 + jnp.exp(-pre))
        act[:, cols] = (pre * sig * live).astype(BF16)
        dpre = cot[:, cols].astype(F32) * live * sig * (1.0 + pre * (1.0 - sig))
        part = jnp.sum(dpre * inner, axis=0, keepdims=True)
        for h in range(2):
            for r in range(3):
                at = h * 384 + r * 128
                sbuf[n * 2 + h, r : r + 1, :] = part[:, at : at + 128]
        dinner[:, cols] = (dpre * sc).astype(BF16)
        return 0

    lax.fori_loop(0, 4, forward, 0)

    nt = (((1,), (1,)), ((), ()))

    def backward_v(n, _):
        rows = pl.ds(pl.multiple_of(n * 256, 256), 256)
        vbuf[:, rows] = lax.dot_general(dinner[...], deq[rows, :], nt, preferred_element_type=F32).astype(BF16)
        return 0

    lax.fori_loop(0, 6, backward_v, 0)

    def backward_n(n, _):
        rows = pl.ds(pl.multiple_of(n * 512, 512), 512)
        dnorm[:, rows] = lax.dot_general(vbuf[...], rfull[rows, :], nt, preferred_element_type=F32)
        return 0

    lax.fori_loop(0, 3, backward_n, 0)

    dn = dnorm[...]
    xh = xhat[...]
    gpart = jnp.sum(dn * xh, axis=0, keepdims=True)
    for r in range(12):
        gbuf[3 + r : 4 + r, :] = gpart[:, r * 128 : (r + 1) * 128]
    msg_a[...] = sbuf[...] + gbuf[...][None]
    got_a[fs] = msg_a[fs]

    def red_a(j, _):
        pf = (fs + j) % NF
        to(msg_a.at[pf], got_a.at[fs], s_red.at[0], r_red.at[0], dp, pf).start()
        return 0

    lax.fori_loop(1, NF, red_a, 0)

    dx = dn * gain[...]
    m1 = jnp.sum(dx, axis=1, keepdims=True) * (1.0 / D)
    m2 = jnp.sum(dx * xh, axis=1, keepdims=True) * (1.0 / D)
    mfg[...] = (inv * (dx - m1 - xh * m2)).astype(BF16)

    wait_for(got_a.at[0 : NF - 1], r_red.at[0])
    total = jnp.sum(got_a[...], axis=0)
    msg_b[...] = total
    got_b[xy] = total

    def red_b(j, _):
        to(msg_b, got_b.at[xy], s_red.at[1], r_red.at[1], zlo * 16 + (xy + j) % 16, fs).start()
        return 0

    lax.fori_loop(1, 16, red_b, 0)
    wait_for(got_b.at[0:15], r_red.at[1])
    total = jnp.sum(got_b[...], axis=0)
    msg_c[...] = total
    got_c[zlo] = total
    for j in (1, 2, 3):
        to(msg_c, got_c.at[zlo], s_red.at[2], r_red.at[2], ((zlo + j) % 4) * 16 + xy, fs).start()
    wait_for(got_c.at[0:3], r_red.at[2])
    red[...] = jnp.sum(got_c[...], axis=0)

    wait_for(outb.at[0 : (NDP - 1) * MSG, :], s_frames)
    wait_for(wout.at[0 : NDP - 1], s_meta)
    for k in range(3):
        wait_for(cpk, s_code.at[k])
        wait_for(piece(fs, xx, yy), s_r0.at[k])
    for k in range(4):
        wait_for(cpk, s_codex.at[k])
        wait_for(rfull.at[0:192, :], s_rx.at[k])
    wait_for(rfull.at[0:432, 0:PC], s_r1)
    wait_for(rfull.at[0:432, :], s_r2)
    wait_for(got_a.at[0 : NF - 1], s_red.at[0])
    wait_for(got_b.at[0:15], s_red.at[1])
    wait_for(got_c.at[0:3], s_red.at[2])


def body(
    frames, frame_mask, block_dest, codes_first, codes_second, codebook_first, codebook_second,
    rotation, gain, scale, cotangent,
):
    drow = jnp.repeat(block_dest, 4)[None, :]
    mrow = frame_mask.astype(F32)[None, :]
    both = jnp.concatenate([codes_first.T, codes_second.T, jnp.zeros((2, D), jnp.int32)], axis=0)
    cpk = both.astype(BF16).reshape(8, 12, 128).transpose(1, 0, 2).reshape(96, 128)
    dma = pltpu.SemaphoreType.DMA
    vm = pltpu.VMEM
    act, mfg, red = pl.pallas_call(
        kernel,
        out_shape=(
            jax.ShapeDtypeStruct((ROWS, FF), BF16),
            jax.ShapeDtypeStruct((ROWS, D), BF16),
            jax.ShapeDtypeStruct((16, 128), F32),
        ),
        in_specs=[pl.BlockSpec(memory_space=pltpu.VMEM)] * 10,
        out_specs=(pl.BlockSpec(memory_space=pltpu.VMEM),) * 3,
        scratch_shapes=[
            vm((NDP * MSG, SEG), BF16), vm((NDP * MSG, SEG), BF16),
            vm((NDP, 1, ROWS), F32), vm((NDP, 1, ROWS), F32),
            vm((NF, 96, 128), BF16), vm((128, 128), F32), vm((512, 256), BF16),
            vm((D, D), BF16), vm((D, FF), BF16),
            vm((ROWS, D), F32), vm((ROWS, D), BF16), vm((ROWS, D), BF16),
            vm((ROWS, FF), BF16), vm((ROWS, D), BF16), vm((ROWS, D), F32),
            vm((NF, 16, 128), F32), vm((16, 128), F32),
            vm((NF, 16, 128), F32), vm((NF, 16, 128), F32),
            vm((16, 128), F32), vm((16, 16, 128), F32),
            vm((16, 128), F32), vm((4, 16, 128), F32),
            dma, dma, dma, dma, dma,
            dma((3,)), dma((3,)), dma((4,)), dma((4,)),
            dma((3,)), dma((3,)), dma, dma((3,)), dma, dma((3,)), dma((4,)), dma((4,)),
            dma((3,)), dma((3,)),
        ],
        compiler_params=pltpu.CompilerParams(
            collective_id=0, has_side_effects=True, vmem_limit_bytes=52 * 1024 * 1024
        ),
        cost_estimate=pl.CostEstimate(flops=14_000_000_000, bytes_accessed=8_000_000, transcendentals=400_000),
    )(
        frames, drow, mrow, cpk, codebook_first, codebook_second, rotation,
        gain[None, :], scale[None, :], cotangent,
    )
    return act, mfg, red[0:3].reshape(384), red[3:15].reshape(D)


def solution(mesh):
    rows = P(("dp", "fsdp"), None)
    flat = P(("dp", "fsdp"))
    placed = (
        rows, flat, flat, P(None, "fsdp"), P(None, "fsdp"), P(), P(), P("fsdp", None), P(), P(), rows,
    )
    return jax.shard_map(
        body,
        mesh=mesh,
        in_specs=placed,
        out_specs=(rows, rows, P("fsdp"), P()),
        check_vma=False,
    )
```

time: 658 us -> 104 us (0.16)
  the two profiles are of different devices: /device:TPU:8 before, /device:TPU:1 now
where the time goes in v1:
time: 104 us; the launch traced here: 103 us
  Pallas kernels  91.8 us (88%)
  local copies, waits for them, and re-layouts  9.19 us (9%)
  other arithmetic  1.54 us (1%)
    pallas_call x1, Pallas kernels, body(): pl.pallas_call(kernel, out_shape=(jax.ShapeDtypeStruct((ROWS, FF), BF16),...  91.8 us
    unnamed x12, local copies, waits for them, and re-layouts  6.4 us

profile of v1, /device:TPU:1, one launch (start us, length us, event | category | flops | bytes accessed | tf_op | source)
XLA Modules:
  0.0 103.2 jit_solution(18068541998310406514)
XLA Ops:
  0.6 0.0 copy-start.2
  0.6 0.7 convert_bitcast_fusion.2.mrow
  1.3 0.1 pad.2.clone
  1.4 0.7 broadcast_in_dim.18.gain
  2.1 0.7 broadcast_in_dim.15
  2.8 0.1 broadcast_in_dim_reshape.3.drow
  2.9 0.8 convert_bitcast_fusion
  3.7 0.0 copy-start.4
  3.7 0.1 maximum_bitcast_fusion.cpk
  3.8 0.0 copy-done.2
  3.8 0.6 copy-done.4
  4.4 0.0 copy-start
  4.4 1.1 %copy-done = bf16[192,1536]{1,0:T(8,128)(2,1)S(1)} copy-done((bf16[192,1536]{1,0:T(8,128)(2,1)S(1)}, bf16[192,1536]{1,0:T(8,128)(2,1)}, u32[]{:S(2)}) %copy-start) | copy-done | bytes 589848
  5.5 0.0 copy-start.1
  5.5 1.0 copy-done.1
  6.5 0.0 copy-start.3
  6.5 0.9 copy-done.3
  7.4 91.8 %shard_map.138 = (bf16[128,3072]{1,0:T(8,128)(2,1)}, bf16[128,1536]{1,0:T(8,128)(2,1)S(1)}, f32[16,128]{1,0:T(8,128)S(1)}) custom-call(bf16[128,1536]{1,0:T(8,128)(2,1)S(1)} %copy-done.1, s32[1,128]{1,0:T(1,128)S(1)} %broadcast_in_dim_reshape.3.drow, f32[1,128]{1,0:T(1,128)S(1)} %convert_bitcast_fusion.2.mrow, bf16[96,128]{1,0:T(8,128)(2,1)S(1)} %maximum_bitcast_fusion.cpk, ...), custom_call_target="tpu_custom_call" | custom-call | flops 14000000000 | bytes 8000000 | tf_op jit(solution)/shard_map/pallas_call | solution.py:335
  99.2 0.6 slice_bitcast_fusion.1
  99.7 0.6 slice_bitcast_fusion
  100.3 2.1 %copy.21 = bf16[128,3072]{1,0:T(8,128)(2,1)} copy(bf16[128,3072]{1,0:T(8,128)(2,1)} %get-tuple-element.16) | data formatting | bytes 1572864
  102.4 0.7 copy.22
  (1 shorter events, 0.0 us)
Async XLA Ops:
  0.6 3.2 %copy-start.2 = (f32[256,128]{1,0:T(8,128)S(1)}, f32[256,128]{1,0:T(8,128)}, u32[]{:S(2)}) copy-start(f32[256,128]{1,0:T(8,128)} %cb1.1) | copy-start | bytes 393220
  3.7 0.7 copy-start.4
  4.4 1.1 %copy-start = (bf16[192,1536]{1,0:T(8,128)(2,1)S(1)}, bf16[192,1536]{1,0:T(8,128)(2,1)}, u32[]{:S(2)}) copy-start(bf16[192,1536]{1,0:T(8,128)(2,1)} %rot.1) | copy-start | bytes 1769476
  5.5 1.0 copy-start.1
  6.5 0.9 copy-start.3

commit v2 on v1

v2 whole, which is shorter than its diff:
```python
import jax
import jax.numpy as jnp
from jax import lax
from jax.experimental import pallas as pl
from jax.experimental.pallas import tpu as pltpu
from jax.sharding import PartitionSpec as P

MESH = pl.DeviceIdType.MESH
F32 = jnp.float32
BF16 = jnp.bfloat16
NDP, NF = 64, 8
ROWS, D, FF = 128, 1536, 3072
SEG = 384
MSG = 16
PR, PC = 48, 384
HALF = D // 2
WIDE = 768


def iota(shape, dim, dtype=jnp.int32):
    found = lax.broadcasted_iota(jnp.int32, shape, dim)
    return found if dtype == jnp.int32 else found.astype(dtype)


def kernel(
    frames_h, mask_h, dest_h, c1_h, c2_h, cb1_h, cb2_h, rot_h, gain_h, scale_h, cot_h,
    act_h, mfg_h, sred, gred,
    frames, mask, destv, c1, c2, cb1, cb2, gain, scale, cot, act, mfg,
    outb, inb, wout, win, codef, codes, cbcat, rfull, deq, xhat, normed, ubuf, vacc, vbuf, dnorm,
    sbuf, sgot, smsg_b, sgot_b, smsg_c, sgot_c, ghalf, ggot, gmsg_z, ggot_z, gmsg_x, ggot_x, gfin,
    s_in, s_out, s_frames, r_frames, s_meta, r_meta, s_own, s_c0, r_c0, s_c1, r_c1,
    s_r0, r_r0, s_r1, r_r1, s_r2, r_r2, s_rx, r_rx, s_dx, r_dx, s_red, r_red,
):
    dp = lax.axis_index("dp")
    fs = lax.axis_index("fsdp")
    zlo, xy = dp // 16, dp % 16
    xx, yy = xy // 4, xy % 4
    zhi, core = fs // 2, fs % 2
    zz = zhi * 4 + zlo
    other = zhi * 2 + 1 - core

    def to(src, dst, send, recv, d, f):
        return pltpu.make_async_remote_copy(
            src_ref=src, dst_ref=dst, send_sem=send, recv_sem=recv,
            device_id=(d, f), device_id_type=MESH,
        )

    def wait_for(ref, sem):
        pltpu.make_async_copy(ref, ref, sem).wait()

    def rows_of(f):
        return pl.ds(pl.multiple_of(f * 192, 192), 192)

    def cols_of(f):
        return pl.ds(pl.multiple_of(f * SEG, SEG), SEG)

    pairs = (
        (dest_h, destv), (mask_h, mask), (frames_h, frames), (c1_h, c1), (c2_h, c2), (cb1_h, cb1), (cb2_h, cb2),
        (gain_h, gain), (scale_h, scale), (cot_h, cot), (rot_h, rfull.at[rows_of(fs), :]),
    )
    loads = [pltpu.make_async_copy(a, b, s_in.at[n]) for n, (a, b) in enumerate(pairs)]
    for load in loads:
        load.start()

    barrier = pltpu.get_barrier_semaphore()

    def greet(d, f):
        pl.semaphore_signal(barrier, inc=1, device_id=(d, f), device_id_type=MESH)

    def hello_dp(j, _):
        greet((dp + j) % NDP, fs)
        return 0

    def hello_fs(j, _):
        greet(dp, (fs + j) % NF)
        return 0

    def hello_z(j, _):
        greet(((zlo + 1 + j % 3) % 4) * 16 + xy, ((zhi + 1 + j // 3) % 4) * 2 + core)
        return 0

    lax.fori_loop(1, NF, hello_fs, 0)
    lax.fori_loop(1, NDP, hello_dp, 0)
    lax.fori_loop(0, 9, hello_z, 0)

    codef[...] = jnp.zeros_like(codef)
    loads[3].wait()
    loads[4].wait()
    for t in range(12):
        codef[t * 8 : t * 8 + 3, :] = c1[:, t * 128 : (t + 1) * 128].astype(F32)
        codef[t * 8 + 3 : t * 8 + 6, :] = c2[:, t * 128 : (t + 1) * 128].astype(F32)
    codes[fs] = codef[...].astype(BF16)

    loads[0].wait()
    loads[1].wait()
    spread4 = jnp.where(iota((32, ROWS), 1) // 4 == iota((32, ROWS), 0), 1.0, 0.0).astype(BF16)
    dest8 = jnp.broadcast_to(destv[...].reshape(1, 32).astype(F32), (8, 32)).astype(BF16)
    dest = jnp.dot(dest8, spread4, preferred_element_type=F32)[0:1, :].astype(jnp.int32)
    mask_in = mask[...].reshape(1, ROWS).astype(F32)
    lane = iota((1, ROWS), 1)
    key = jnp.concatenate([dest * MSG + s * 4 + lane % 4 for s in range(4)], axis=1)
    wout[...] = jnp.where(iota((NDP, 1, ROWS), 0) == dest[None], 1.0 + mask_in[None], 0.0)
    win[dp] = wout[dp]
    loads[2].wait()
    wide = jnp.concatenate([frames[:, s * SEG : (s + 1) * SEG] for s in range(4)], axis=0)

    def fill(k, _):
        row = iota((256, 4 * ROWS), 0) + k * 256
        pick = jnp.where(row == key, 1.0, 0.0).astype(BF16)
        outb[pl.ds(pl.multiple_of(k * 256, 256), 256), :] = jnp.dot(
            pick, wide, preferred_element_type=F32
        ).astype(BF16)
        return 0

    lax.fori_loop(0, 4, fill, 0)

    pl.semaphore_wait(barrier, NDP - 1 + NF - 1 + 9)

    def piece(f, i, j):
        return rfull.at[
            pl.ds(pl.multiple_of(f * 192 + i * PR, 16), PR), pl.ds(pl.multiple_of(j * PC, 128), PC)
        ]

    def own_piece(i, j):
        return rot_h.at[pl.ds(pl.multiple_of(i * PR, 16), PR), pl.ds(pl.multiple_of(j * PC, 128), PC)]

    def code_piece(f, i):
        return codes.at[f, pl.ds(pl.multiple_of(i * 32, 32), 32), :]

    def away(k):
        return ((zhi + k) % 4) * 2 + core

    def back(k):
        return ((zhi + 4 - k) % 4) * 2 + core

    def other_of(f):
        return f + 1 - 2 * core

    for k in (1, 2, 3):
        to(code_piece(fs, xx), code_piece(fs, xx), s_c0.at[k - 1], r_c0.at[k - 1], dp, away(k)).start()
    for k in (1, 2, 3):
        to(own_piece(xx, yy), piece(fs, xx, yy), s_r0.at[k - 1], r_r0.at[k - 1], dp, away(k)).start()
    to(rot_h, rfull.at[rows_of(fs), :], s_rx.at[0], r_rx.at[0], dp, other).start()

    def block(c):
        return pl.ds(pl.multiple_of(c * MSG, MSG), MSG)

    def send_block(j, _):
        peer = (dp + j) % NDP
        to(wout.at[peer], win.at[dp], s_meta, r_meta, peer, fs).start()
        to(outb.at[block(peer), :], inb.at[block(dp), :], s_frames, r_frames, peer, fs).start()
        return 0

    lax.fori_loop(1, 22, send_block, 0)
    own = pltpu.make_async_copy(outb.at[block(dp), :], inb.at[block(dp), :], s_own)
    own.start()

    for k, (n, book) in enumerate(((5, cb1), (6, cb2))):
        loads[n].wait()
        value = book[...]
        high = value.astype(BF16)
        cbcat[k * 256 : (k + 1) * 256, 0:128] = high
        cbcat[k * 256 : (k + 1) * 256, 128:256] = (value - high.astype(F32)).astype(BF16)

    def look_up(f, n):
        table = codes[f].astype(F32).T
        entry = iota((128, 256), 1, F32)

        def hot(c):
            return jnp.where(table[:, c : c + 1] == entry, 1.0, 0.0).astype(BF16)

        hots = jnp.concatenate(
            [
                jnp.concatenate([hot(t * 8 + q), hot(t * 8 + 3 + q)], axis=1)
                for t in range(12)
                for q in range(3)
            ],
            axis=0,
        )
        found = jnp.dot(hots, cbcat[...], preferred_element_type=F32)
        found = (found[:, :128] + found[:, 128:]).astype(BF16)
        for t in range(12):
            for q in range(3):
                at = (t * 3 + q) * 128
                deq[t * 128 : (t + 1) * 128, pl.ds(pl.multiple_of(f * SEG + q * 128, 128), 128)] = found[at : at + 128]
        to(deq.at[:, cols_of(f)], deq.at[:, cols_of(f)], s_dx.at[n], r_dx.at[n], dp, other).start()

    look_up(fs, 0)

    for k in (1, 2, 3):
        wait_for(code_piece(back(k), xx), r_c0.at[k - 1])
        for d in (1, 2, 3):
            peer = zlo * 16 + ((xx + d) % 4) * 4 + yy
            to(code_piece(back(k), xx), code_piece(back(k), xx), s_c1, r_c1.at[k - 1], peer, fs).start()
    for k in (1, 2, 3):
        wait_for(piece(back(k), xx, yy), r_r0.at[k - 1])
        for d in (1, 2, 3):
            nx = (xx + d * (1 - core)) % 4
            ny = (yy + d * core) % 4
            to(piece(back(k), xx, yy), piece(back(k), xx, yy), s_r1, r_r1.at[k - 1], zlo * 16 + nx * 4 + ny, fs).start()

    lax.fori_loop(22, 43, send_block, 0)

    for k in (1, 2):
        wait_for(codes.at[0, 0:96, :], r_c1.at[k - 1])
        look_up(back(k), k)

    for k in (1, 2, 3):
        wait_for(rfull.at[0:144, 0:PC], r_r1.at[k - 1])

        def spread(n, _):
            d, m = n // 4 + 1, n % 4
            nx = (xx + d * core) % 4
            ny = (yy + d * (1 - core)) % 4
            px = m * (1 - core) + xx * core
            py = yy * (1 - core) + m * core
            to(piece(back(k), px, py), piece(back(k), px, py), s_r2, r_r2.at[k - 1], zlo * 16 + nx * 4 + ny, fs).start()
            return 0

        lax.fori_loop(0, 12, spread, 0)

    lax.fori_loop(43, NDP, send_block, 0)

    wait_for(codes.at[0, 0:96, :], r_c1.at[2])
    look_up(back(3), 3)
    loads[10].wait()

    for k in (1, 2, 3):
        wait_for(rfull.at[0:576, 0:PC], r_r2.at[k - 1])
        to(rfull.at[rows_of(back(k)), :], rfull.at[rows_of(back(k)), :], s_rx.at[k], r_rx.at[k], dp, other).start()

    wait_for(win.at[0 : NDP - 1], r_meta)
    wait_for(inb.at[0 : (NDP - 1) * MSG, :], r_frames)
    own.wait()
    meta = win[...]
    mask_row = jnp.sum(meta, axis=0) - 1.0
    src_row = jnp.sum(jnp.where(meta > 0.5, iota((NDP, 1, ROWS), 0, F32), 0.0), axis=0)
    eye = iota((ROWS, ROWS), 0) == iota((ROWS, ROWS), 1)
    live = jnp.sum(jnp.where(eye, mask_row, 0.0), axis=1, keepdims=True)
    src = jnp.sum(jnp.where(eye, src_row, 0.0), axis=1, keepdims=True)
    first = src * float(MSG) + (iota((ROWS, 1), 0) % 4).astype(F32)
    for s in range(4):
        put = jnp.where(iota((ROWS, NDP * MSG), 1, F32) == first + 4.0 * s, 1.0, 0.0).astype(BF16)
        xhat[:, s * SEG : (s + 1) * SEG] = jnp.dot(put, inb[...], preferred_element_type=F32)
    xval = xhat[...]
    centered = xval - jnp.sum(xval, axis=1, keepdims=True) * (1.0 / D)
    inv = lax.rsqrt(jnp.sum(centered * centered, axis=1, keepdims=True) * (1.0 / D) + 1e-06)
    standard = centered * inv
    xhat[...] = standard
    loads[7].wait()
    gain_row = gain[...].reshape(1, D)
    normed[...] = (standard * gain_row).astype(BF16)

    for k in range(4):
        wait_for(rfull.at[rows_of(other_of(back(k))), :], r_rx.at[k])

    def forward_u(n, _):
        cols = pl.ds(pl.multiple_of(n * 512, 512), 512)
        ubuf[:, cols] = jnp.dot(normed[...], rfull[:, cols], preferred_element_type=F32).astype(BF16)
        return 0

    lax.fori_loop(0, 3, forward_u, 0)

    loads[8].wait()
    loads[9].wait()
    for k in range(4):
        wait_for(deq.at[:, cols_of(other_of(back(k)))], r_dx.at[k])
    vacc[...] = jnp.zeros_like(vacc)
    nt = (((1,), (1,)), ((), ()))
    for n in range(FF // WIDE):
        cols = slice(n * WIDE, (n + 1) * WIDE)
        inner = jnp.dot(ubuf[...], deq[:, cols], preferred_element_type=F32)
        sc = scale[:, cols]
        pre = inner * sc
        sig = 1.0 / (1.0 + jnp.exp(-pre))
        act[:, cols] = (pre * sig * live).astype(BF16)
        dpre = cot[:, cols].astype(F32) * live * sig * (1.0 + pre * (1.0 - sig))
        part = jnp.sum(dpre * inner, axis=0, keepdims=True)
        sbuf[2 * n] = part[:, :SEG]
        sbuf[2 * n + 1] = part[:, SEG:]
        dinner = (dpre * sc).astype(BF16)
        vacc[...] += lax.dot_general(dinner, deq[:, cols], nt, preferred_element_type=F32)

    sgot[fs] = sbuf[fs]

    def sums_a(j, _):
        pf = (fs + j) % NF
        to(sbuf.at[pf], sgot.at[fs], s_red.at[0], r_red.at[0], dp, pf).start()
        return 0

    lax.fori_loop(1, NF, sums_a, 0)
    act_out = pltpu.make_async_copy(act, act_h, s_out.at[0])
    act_out.start()

    vbuf[...] = vacc[...].astype(BF16)

    def backward_n(n, _):
        rows = pl.ds(pl.multiple_of(n * 512, 512), 512)
        dnorm[:, rows] = lax.dot_general(vbuf[...], rfull[rows, :], nt, preferred_element_type=F32)
        return 0

    lax.fori_loop(0, 3, backward_n, 0)

    dn = dnorm[...]
    xh = xhat[...]
    gpart = jnp.sum(dn * xh, axis=0, keepdims=True)
    ghalf[0] = gpart[:, :HALF]
    ghalf[1] = gpart[:, HALF:]
    to(ghalf.at[1 - core], ggot, s_red.at[3], r_red.at[3], dp, other).start()

    wait_for(sgot.at[0 : NF - 1], r_red.at[0])
    total = jnp.sum(sgot[...], axis=0)
    smsg_b[...] = total
    sgot_b[xy] = total

    def sums_b(j, _):
        to(smsg_b, sgot_b.at[xy], s_red.at[1], r_red.at[1], zlo * 16 + (xy + j) % 16, fs).start()
        return 0

    lax.fori_loop(1, 16, sums_b, 0)

    wait_for(ggot, r_red.at[3])
    total = ghalf[core] + ggot[...]
    gmsg_z[...] = total
    ggot_z[zz] = total

    def gains_z(j, _):
        pz = (zz + j) % 16
        to(gmsg_z, ggot_z.at[zz], s_red.at[4], r_red.at[4], (pz % 4) * 16 + xy, (pz // 4) * 2 + core).start()
        return 0

    lax.fori_loop(1, 16, gains_z, 0)

    dx = dn * gain_row
    m1 = jnp.sum(dx, axis=1, keepdims=True) * (1.0 / D)
    m2 = jnp.sum(dx * xh, axis=1, keepdims=True) * (1.0 / D)
    mfg[...] = (inv * (dx - m1 - xh * m2)).astype(BF16)
    mfg_out = pltpu.make_async_copy(mfg, mfg_h, s_out.at[1])
    mfg_out.start()

    wait_for(ggot_z.at[0:15], r_red.at[4])
    total = jnp.sum(ggot_z[...], axis=0)
    gmsg_x[...] = total
    ggot_x[xy] = total

    def gains_x(j, _):
        to(gmsg_x, ggot_x.at[xy], s_red.at[5], r_red.at[5], zlo * 16 + (xy + j) % 16, fs).start()
        return 0

    lax.fori_loop(1, 16, gains_x, 0)

    wait_for(sgot_b.at[0:15], r_red.at[1])
    total = jnp.sum(sgot_b[...], axis=0)
    smsg_c[...] = total
    sgot_c[zlo] = total
    for j in (1, 2, 3):
        to(smsg_c, sgot_c.at[zlo], s_red.at[2], r_red.at[2], ((zlo + j) % 4) * 16 + xy, fs).start()

    wait_for(ggot_x.at[0:15], r_red.at[5])
    gfin[core] = jnp.sum(ggot_x[...], axis=0)
    to(gfin.at[core], gfin.at[core], s_red.at[6], r_red.at[6], dp, other).start()

    wait_for(outb.at[0 : (NDP - 1) * MSG, :], s_frames)
    wait_for(wout.at[0 : NDP - 1], s_meta)
    for k in range(3):
        wait_for(code_piece(fs, xx), s_c0.at[k])
        wait_for(own_piece(xx, yy), s_r0.at[k])
    wait_for(codes.at[0:3, 0:96, :], s_c1)
    for k in range(4):
        wait_for(rfull.at[0:192, :], s_rx.at[k])
        wait_for(deq.at[:, 0:SEG], s_dx.at[k])
    wait_for(rfull.at[0:432, 0:PC], s_r1)
    wait_for(rfull.at[0:432, :], s_r2)
    wait_for(sgot.at[0 : NF - 1], s_red.at[0])
    wait_for(sgot_b.at[0:15], s_red.at[1])
    wait_for(ghalf.at[0], s_red.at[3])
    wait_for(ggot_z.at[0:15], s_red.at[4])
    wait_for(ggot_x.at[0:15], s_red.at[5])
    act_out.wait()
    mfg_out.wait()

    wait_for(sgot_c.at[0:3], r_red.at[2])
    sred[...] = jnp.sum(sgot_c[...], axis=0)
    wait_for(sgot_c.at[0:3], s_red.at[2])
    wait_for(gfin.at[0], r_red.at[6])
    gred[:, :HALF] = gfin[0]
    gred[:, HALF:] = gfin[1]
    wait_for(gfin.at[0], s_red.at[6])


def finish(act, mfg, sred, gred, act_o, mfg_o, s_o, g_o, sems):
    copies = []
    for n in range(4):
        copies.append(pltpu.make_async_copy(act.at[n * 32 : (n + 1) * 32], act_o.at[n * 32 : (n + 1) * 32], sems.at[n]))
    for n in range(2):
        copies.append(pltpu.make_async_copy(mfg.at[n * 64 : (n + 1) * 64], mfg_o.at[n * 64 : (n + 1) * 64], sems.at[4 + n]))
    for copy in copies:
        copy.start()
    s_o[...] = sred[...].reshape(384)
    g_o[...] = gred[...].reshape(D)
    for copy in copies:
        copy.wait()


def body(
    frames, frame_mask, block_dest, codes_first, codes_second, codebook_first, codebook_second,
    rotation, gain, scale, cotangent,
):
    dma = pltpu.SemaphoreType.DMA
    vm = pltpu.VMEM
    shape = jax.ShapeDtypeStruct
    hbm = pl.BlockSpec(memory_space=pltpu.HBM)
    vmem = pl.BlockSpec(memory_space=pltpu.VMEM)
    act, mfg, sred, gred = pl.pallas_call(
        kernel,
        out_shape=(shape((ROWS, FF), BF16), shape((ROWS, D), BF16), shape((1, 384), F32), shape((1, D), F32)),
        in_specs=[hbm] * 11,
        out_specs=(hbm, hbm, vmem, vmem),
        scratch_shapes=[
            vm((ROWS, D), BF16), vm((ROWS,), jnp.int32), vm((32,), jnp.int32),
            vm((3, D), jnp.int32), vm((3, D), jnp.int32), vm((256, 128), F32), vm((256, 128), F32),
            vm((D,), F32), vm((1, FF), F32), vm((ROWS, FF), BF16), vm((ROWS, FF), BF16), vm((ROWS, D), BF16),
            vm((NDP * MSG, SEG), BF16), vm((NDP * MSG, SEG), BF16),
            vm((NDP, 1, ROWS), F32), vm((NDP, 1, ROWS), F32),
            vm((128, 128), F32), vm((NF, 128, 128), BF16), vm((512, 256), BF16),
            vm((D, D), BF16), vm((D, FF), BF16),
            vm((ROWS, D), F32), vm((ROWS, D), BF16), vm((ROWS, D), BF16),
            vm((ROWS, D), F32), vm((ROWS, D), BF16), vm((ROWS, D), F32),
            vm((NF, 1, SEG), F32), vm((NF, 1, SEG), F32),
            vm((1, SEG), F32), vm((16, 1, SEG), F32), vm((1, SEG), F32), vm((4, 1, SEG), F32),
            vm((2, 1, HALF), F32), vm((1, HALF), F32), vm((1, HALF), F32), vm((16, 1, HALF), F32),
            vm((1, HALF), F32), vm((16, 1, HALF), F32), vm((2, 1, HALF), F32),
            dma((11,)), dma((2,)), dma, dma, dma, dma, dma, dma((3,)), dma((3,)), dma, dma((3,)),
            dma((3,)), dma((3,)), dma, dma((3,)), dma, dma((3,)), dma((4,)), dma((4,)), dma((4,)), dma((4,)),
            dma((7,)), dma((7,)),
        ],
        compiler_params=pltpu.CompilerParams(
            collective_id=0, has_side_effects=True, vmem_limit_bytes=56 * 1024 * 1024
        ),
        cost_estimate=pl.CostEstimate(flops=9_000_000_000, bytes_accessed=8_000_000, transcendentals=400_000),
    )(
        frames, frame_mask, block_dest, codes_first.T, codes_second.T, codebook_first, codebook_second, rotation,
        gain, scale[None, :], cotangent,
    )
    return pl.pallas_call(
        finish,
        out_shape=(shape((ROWS, FF), BF16), shape((ROWS, D), BF16), shape((384,), F32), shape((D,), F32)),
        in_specs=[hbm, hbm, vmem, vmem],
        out_specs=(hbm, hbm, vmem, vmem),
        scratch_shapes=[dma((6,))],
    )(act, mfg, sred, gred)


def solution(mesh):
    rows = P(("dp", "fsdp"), None)
    flat = P(("dp", "fsdp"))
    placed = (
        rows, flat, flat, P(None, "fsdp"), P(None, "fsdp"), P(), P(), P("fsdp", None), P(), P(), rows,
    )
    return jax.shard_map(
        body,
        mesh=mesh,
        in_specs=placed,
        out_specs=(rows, rows, P("fsdp"), P()),
        check_vma=False,
    )
```

time: 104 us -> 124 us (1.19)
  Pallas kernels: 91.8 us -> 123 us
  local copies, waits for them, and re-layouts: 9.19 us -> 0 us
  other arithmetic: 1.54 us -> 0 us
    pallas_call x1 -> x2, Pallas kernels: 91.8 us -> 123 us  [the longest x1 84.8 us: body(): pl.pallas_call(kernel, out_shape=(shape((ROWS, FF), BF16), shape((ROWS, D...]
    unnamed x12 -> x0, local copies, waits for them, and re-layouts: 6.4 us -> none
    broadcast_in_dim x3 -> x0, local copies, waits for them, and re-layouts: 1.43 us -> none  [the longest x1 0.72 us: body(): drow = jnp.repeat(block_dest, 4)[None, :]]
where the time goes in v2:
time: 124 us
  Pallas kernels  123 us (99%)
    pallas_call x1, Pallas kernels, body(): pl.pallas_call(kernel, out_shape=(shape((ROWS, FF), BF16), shape((ROWS, D...  84.8 us
    pallas_call x1, Pallas kernels, body(): pl.pallas_call(finish, out_shape=(shape((ROWS, FF), BF16), shape((ROWS, D...  38.2 us

profile of v2, /device:TPU:1, one launch (start us, length us, event | category | flops | bytes accessed | tf_op | source)
XLA Modules:
  0.0 123.7 jit_solution(12533252970064407098)
XLA Ops:
  0.6 84.8 %shard_map.138 = (bf16[128,3072]{1,0:T(8,128)(2,1)}, bf16[128,1536]{1,0:T(8,128)(2,1)}, f32[1,384]{1,0:T(1,128)}, f32[1,1536]{1,0:T(1,128)}) custom-call(bf16[128,1536]{1,0:T(8,128)(2,1)} %frames_h.1, s32[128]{0:T(128)} %mask_h.1, s32[32]{0:T(128)} %dest_h.1, s32[3,1536]{1,0:T(4,128)} %bitcast.3, s32[3,1536]{1,0:T(4,128)} %bitcast.4, f32[256,128]{1,0:T(8,128)} %cb1_h.1, ...), custom_call_target="tpu_custom_call" | custom-call | flops 8999999488 | bytes 8000000 | tf_op jit(solution)/shard_map/pallas_call | solution.py:414
  85.4 38.2 %shard_map.139 = (bf16[128,3072]{1,0:T(8,128)(2,1)}, bf16[128,1536]{1,0:T(8,128)(2,1)}, f32[384]{0:T(512)}, f32[1536]{0:T(1024)}) custom-call(bf16[128,3072]{1,0:T(8,128)(2,1)} %get-tuple-element.8.act, bf16[128,1536]{1,0:T(8,128)(2,1)} %get-tuple-element.9.mfg, f32[1,384]{1,0:T(1,128)} %get-tuple-element.10.sred, f32[1,1536]{1,0:T(1,128)} %get-tuple-element.11.gred), custom_call_target="tpu_custom_call" | custom-call | tf_op jit(solution)/shard_map/pallas_call | solution.py:445

commit v3 on v2

--- a/solution.py
+++ b/solution.py
@@ -27,7 +27,7 @@
     act_h, mfg_h, sred, gred,
     frames, mask, destv, c1, c2, cb1, cb2, gain, scale, cot, act, mfg,
     outb, inb, wout, win, codef, codes, cbcat, rfull, deq, xhat, normed, ubuf, vacc, vbuf, dnorm,
-    sbuf, sgot, smsg_b, sgot_b, smsg_c, sgot_c, ghalf, ggot, gmsg_z, ggot_z, gmsg_x, ggot_x, gfin,
+    sbuf, sgot, smsg_b, sgot_b, smsg_c, sgot_c, ghalf, ggot_x, gmsg_z, ggot_z, gfin,
     s_in, s_out, s_frames, r_frames, s_meta, r_meta, s_own, s_c0, r_c0, s_c1, r_c1,
     s_r0, r_r0, s_r1, r_r1, s_r2, r_r2, s_rx, r_rx, s_dx, r_dx, s_red, r_red,
 ):
@@ -82,6 +82,12 @@
     lax.fori_loop(1, NF, hello_fs, 0)
     lax.fori_loop(1, NDP, hello_dp, 0)
     lax.fori_loop(0, 9, hello_z, 0)
+
+    def hello_x(j, _):
+        greet(zlo * 16 + (xy + j) % 16, other)
+        return 0
+
+    lax.fori_loop(1, 16, hello_x, 0)
 
     codef[...] = jnp.zeros_like(codef)
     loads[3].wait()
@@ -114,7 +120,7 @@
 
     lax.fori_loop(0, 4, fill, 0)
 
-    pl.semaphore_wait(barrier, NDP - 1 + NF - 1 + 9)
+    pl.semaphore_wait(barrier, NDP - 1 + NF - 1 + 9 + 15)
 
     def piece(f, i, j):
         return rfull.at[
@@ -136,9 +142,9 @@
     def other_of(f):
         return f + 1 - 2 * core
 
-    for k in (1, 2, 3):
+    for k in (2, 1, 3):
         to(code_piece(fs, xx), code_piece(fs, xx), s_c0.at[k - 1], r_c0.at[k - 1], dp, away(k)).start()
-    for k in (1, 2, 3):
+    for k in (2, 1, 3):
         to(own_piece(xx, yy), piece(fs, xx, yy), s_r0.at[k - 1], r_r0.at[k - 1], dp, away(k)).start()
     to(rot_h, rfull.at[rows_of(fs), :], s_rx.at[0], r_rx.at[0], dp, other).start()
 
@@ -187,29 +193,34 @@
 
     look_up(fs, 0)
 
-    for k in (1, 2, 3):
+    for k in (1, 3, 2):
         wait_for(code_piece(back(k), xx), r_c0.at[k - 1])
         for d in (1, 2, 3):
             peer = zlo * 16 + ((xx + d) % 4) * 4 + yy
             to(code_piece(back(k), xx), code_piece(back(k), xx), s_c1, r_c1.at[k - 1], peer, fs).start()
-    for k in (1, 2, 3):
+    for k in (1, 3, 2):
         wait_for(piece(back(k), xx, yy), r_r0.at[k - 1])
         for d in (1, 2, 3):
             nx = (xx + d * (1 - core)) % 4
             ny = (yy + d * core) % 4
             to(piece(back(k), xx, yy), piece(back(k), xx, yy), s_r1, r_r1.at[k - 1], zlo * 16 + nx * 4 + ny, fs).start()
+        for d in (1, 2, 3):
+            nx = (xx + d * core) % 4
+            ny = (yy + d * (1 - core)) % 4
+            to(piece(back(k), xx, yy), piece(back(k), xx, yy), s_r2, r_r2.at[k - 1], zlo * 16 + nx * 4 + ny, fs).start()
 
     lax.fori_loop(22, 43, send_block, 0)
 
-    for k in (1, 2):
+    for k in (1, 3):
         wait_for(codes.at[0, 0:96, :], r_c1.at[k - 1])
         look_up(back(k), k)
 
-    for k in (1, 2, 3):
+    for k in (1, 3, 2):
         wait_for(rfull.at[0:144, 0:PC], r_r1.at[k - 1])
 
         def spread(n, _):
-            d, m = n // 4 + 1, n % 4
+            d = n // 3 + 1
+            m = (xx * (1 - core) + yy * core + 1 + n % 3) % 4
             nx = (xx + d * core) % 4
             ny = (yy + d * (1 - core)) % 4
             px = m * (1 - core) + xx * core
@@ -217,15 +228,15 @@
             to(piece(back(k), px, py), piece(back(k), px, py), s_r2, r_r2.at[k - 1], zlo * 16 + nx * 4 + ny, fs).start()
             return 0
 
-        lax.fori_loop(0, 12, spread, 0)
+        lax.fori_loop(0, 9, spread, 0)
 
     lax.fori_loop(43, NDP, send_block, 0)
 
-    wait_for(codes.at[0, 0:96, :], r_c1.at[2])
-    look_up(back(3), 3)
+    wait_for(codes.at[0, 0:96, :], r_c1.at[1])
+    look_up(back(2), 2)
     loads[10].wait()
 
-    for k in (1, 2, 3):
+    for k in (1, 3, 2):
         wait_for(rfull.at[0:576, 0:PC], r_r2.at[k - 1])
         to(rfull.at[rows_of(back(k)), :], rfull.at[rows_of(back(k)), :], s_rx.at[k], r_rx.at[k], dp, other).start()
 
@@ -306,30 +317,21 @@
     gpart = jnp.sum(dn * xh, axis=0, keepdims=True)
     ghalf[0] = gpart[:, :HALF]
     ghalf[1] = gpart[:, HALF:]
-    to(ghalf.at[1 - core], ggot, s_red.at[3], r_red.at[3], dp, other).start()
-
-    wait_for(sgot.at[0 : NF - 1], r_red.at[0])
-    total = jnp.sum(sgot[...], axis=0)
-    smsg_b[...] = total
-    sgot_b[xy] = total
-
-    def sums_b(j, _):
-        to(smsg_b, sgot_b.at[xy], s_red.at[1], r_red.at[1], zlo * 16 + (xy + j) % 16, fs).start()
-        return 0
-
-    lax.fori_loop(1, 16, sums_b, 0)
-
-    wait_for(ggot, r_red.at[3])
-    total = ghalf[core] + ggot[...]
-    gmsg_z[...] = total
-    ggot_z[zz] = total
-
-    def gains_z(j, _):
-        pz = (zz + j) % 16
-        to(gmsg_z, ggot_z.at[zz], s_red.at[4], r_red.at[4], (pz % 4) * 16 + xy, (pz // 4) * 2 + core).start()
-        return 0
-
-    lax.fori_loop(1, 16, gains_z, 0)
+    place = core * 16 + xy
+    ggot_x[place] = ghalf[core]
+
+    def gains_x(j, _):
+        peer = zlo * 16 + (xy + j) % 16
+        to(ghalf.at[1 - core], ggot_x.at[place], s_red.at[3], r_red.at[3], peer, other).start()
+        return 0
+
+    def gains_x_own(j, _):
+        peer = zlo * 16 + (xy + j) % 16
+        to(ghalf.at[core], ggot_x.at[place], s_red.at[3], r_red.at[3], peer, fs).start()
+        return 0
+
+    lax.fori_loop(0, 16, gains_x, 0)
+    lax.fori_loop(1, 16, gains_x_own, 0)
 
     dx = dn * gain_row
     m1 = jnp.sum(dx, axis=1, keepdims=True) * (1.0 / D)
@@ -338,16 +340,28 @@
     mfg_out = pltpu.make_async_copy(mfg, mfg_h, s_out.at[1])
     mfg_out.start()
 
-    wait_for(ggot_z.at[0:15], r_red.at[4])
-    total = jnp.sum(ggot_z[...], axis=0)
-    gmsg_x[...] = total
-    ggot_x[xy] = total
-
-    def gains_x(j, _):
-        to(gmsg_x, ggot_x.at[xy], s_red.at[5], r_red.at[5], zlo * 16 + (xy + j) % 16, fs).start()
-        return 0
-
-    lax.fori_loop(1, 16, gains_x, 0)
+    wait_for(sgot.at[0 : NF - 1], r_red.at[0])
+    total = jnp.sum(sgot[...], axis=0)
+    smsg_b[...] = total
+    sgot_b[xy] = total
+
+    def sums_b(j, _):
+        to(smsg_b, sgot_b.at[xy], s_red.at[1], r_red.at[1], zlo * 16 + (xy + j) % 16, fs).start()
+        return 0
+
+    lax.fori_loop(1, 16, sums_b, 0)
+
+    wait_for(ggot_x.at[0:31], r_red.at[3])
+    total = jnp.sum(ggot_x[...], axis=0)
+    gmsg_z[...] = total
+    ggot_z[zz] = total
+
+    def gains_z(j, _):
+        pz = (zz + j) % 16
+        to(gmsg_z, ggot_z.at[zz], s_red.at[4], r_red.at[4], (pz % 4) * 16 + xy, (pz // 4) * 2 + core).start()
+        return 0
+
+    lax.fori_loop(1, 16, gains_z, 0)
 
     wait_for(sgot_b.at[0:15], r_red.at[1])
     total = jnp.sum(sgot_b[...], axis=0)
@@ -355,10 +369,6 @@
     sgot_c[zlo] = total
     for j in (1, 2, 3):
         to(smsg_c, sgot_c.at[zlo], s_red.at[2], r_red.at[2], ((zlo + j) % 4) * 16 + xy, fs).start()
-
-    wait_for(ggot_x.at[0:15], r_red.at[5])
-    gfin[core] = jnp.sum(ggot_x[...], axis=0)
-    to(gfin.at[core], gfin.at[core], s_red.at[6], r_red.at[6], dp, other).start()
 
     wait_for(outb.at[0 : (NDP - 1) * MSG, :], s_frames)
     wait_for(wout.at[0 : NDP - 1], s_meta)
@@ -373,32 +383,42 @@
     wait_for(rfull.at[0:432, :], s_r2)
     wait_for(sgot.at[0 : NF - 1], s_red.at[0])
     wait_for(sgot_b.at[0:15], s_red.at[1])
-    wait_for(ghalf.at[0], s_red.at[3])
-    wait_for(ggot_z.at[0:15], s_red.at[4])
-    wait_for(ggot_x.at[0:15], s_red.at[5])
+    wait_for(ggot_x.at[0:31], s_red.at[3])
     act_out.wait()
     mfg_out.wait()
+
+    wait_for(ggot_z.at[0:15], r_red.at[4])
+    gfin[core] = jnp.sum(ggot_z[...], axis=0)
+    to(gfin.at[core], gfin.at[core], s_red.at[5], r_red.at[5], dp, other).start()
+    wait_for(ggot_z.at[0:15], s_red.at[4])
 
     wait_for(sgot_c.at[0:3], r_red.at[2])
     sred[...] = jnp.sum(sgot_c[...], axis=0)
     wait_for(sgot_c.at[0:3], s_red.at[2])
-    wait_for(gfin.at[0], r_red.at[6])
+    wait_for(gfin.at[0], r_red.at[5])
     gred[:, :HALF] = gfin[0]
     gred[:, HALF:] = gfin[1]
-    wait_for(gfin.at[0], s_red.at[6])
-
-
-def finish(act, mfg, sred, gred, act_o, mfg_o, s_o, g_o, sems):
-    copies = []
+    wait_for(gfin.at[0], s_red.at[5])
+
+
+def finish(act, mfg, sred, gred, act_o, mfg_o, s_o, g_o, act_v, mfg_v, sems):
+    steps = []
     for n in range(4):
-        copies.append(pltpu.make_async_copy(act.at[n * 32 : (n + 1) * 32], act_o.at[n * 32 : (n + 1) * 32], sems.at[n]))
+        at = pl.ds(n * 32, 32)
+        steps.append((act.at[at], act_v.at[at], act_o.at[at]))
     for n in range(2):
-        copies.append(pltpu.make_async_copy(mfg.at[n * 64 : (n + 1) * 64], mfg_o.at[n * 64 : (n + 1) * 64], sems.at[4 + n]))
-    for copy in copies:
+        at = pl.ds(n * 64, 64)
+        steps.append((mfg.at[at], mfg_v.at[at], mfg_o.at[at]))
+    ins = [pltpu.make_async_copy(a, v, sems.at[n]) for n, (a, v, _) in enumerate(steps)]
+    outs = [pltpu.make_async_copy(v, o, sems.at[len(steps) + n]) for n, (_, v, o) in enumerate(steps)]
+    for copy in ins:
         copy.start()
     s_o[...] = sred[...].reshape(384)
     g_o[...] = gred[...].reshape(D)
-    for copy in copies:
+    for arrive, leave in zip(ins, outs):
+        arrive.wait()
+        leave.start()
+    for copy in outs:
         copy.wait()
 
 
@@ -428,11 +448,11 @@
             vm((ROWS, D), F32), vm((ROWS, D), BF16), vm((ROWS, D), F32),
             vm((NF, 1, SEG), F32), vm((NF, 1, SEG), F32),
             vm((1, SEG), F32), vm((16, 1, SEG), F32), vm((1, SEG), F32), vm((4, 1, SEG), F32),
-            vm((2, 1, HALF), F32), vm((1, HALF), F32), vm((1, HALF), F32), vm((16, 1, HALF), F32),
-            vm((1, HALF), F32), vm((16, 1, HALF), F32), vm((2, 1, HALF), F32),
+            vm((2, 1, HALF), F32), vm((32, 1, HALF), F32), vm((1, HALF), F32), vm((16, 1, HALF), F32),
+            vm((2, 1, HALF), F32),
             dma((11,)), dma((2,)), dma, dma, dma, dma, dma, dma((3,)), dma((3,)), dma, dma((3,)),
             dma((3,)), dma((3,)), dma, dma((3,)), dma, dma((3,)), dma((4,)), dma((4,)), dma((4,)), dma((4,)),
-            dma((7,)), dma((7,)),
+            dma((6,)), dma((6,)),
         ],
         compiler_params=pltpu.CompilerParams(
             collective_id=0, has_side_effects=True, vmem_limit_bytes=56 * 1024 * 1024
@@ -447,7 +467,7 @@
         out_shape=(shape((ROWS, FF), BF16), shape((ROWS, D), BF16), shape((384,), F32), shape((D,), F32)),
         in_specs=[hbm, hbm, vmem, vmem],
         out_specs=(hbm, hbm, vmem, vmem),
-        scratch_shapes=[dma((6,))],
+        scratch_shapes=[vm((ROWS, FF), BF16), vm((ROWS, D), BF16), dma((12,))],
     )(act, mfg, sred, gred)
 
 

time: 124 us -> 81 us (0.65)
  Pallas kernels: 123 us -> 80 us
    pallas_call x1, Pallas kernels: 38.2 us -> 3.42 us  [body(): pl.pallas_call(finish, out_shape=(shape((ROWS, FF), BF16), shape((ROWS, D...]
    pallas_call x1, Pallas kernels: 84.8 us -> 76.6 us  [body(): pl.pallas_call(kernel, out_shape=(shape((ROWS, FF), BF16), shape((ROWS, D...]
where the time goes in v3:
time: 81 us; the launch traced here: 80.8 us
  Pallas kernels  80 us (99%)
    pallas_call x1, Pallas kernels, body(): pl.pallas_call(kernel, out_shape=(shape((ROWS, FF), BF16), shape((ROWS, D...  76.6 us
    pallas_call x1, Pallas kernels, body(): pl.pallas_call(finish, out_shape=(shape((ROWS, FF), BF16), shape((ROWS, D...  3.42 us

profile of v3, /device:TPU:1, one launch (start us, length us, event | category | flops | bytes accessed | tf_op | source)
XLA Modules:
  0.0 80.8 jit_solution(16918305282100101155)
XLA Ops:
  0.6 76.6 %shard_map.138 = (bf16[128,3072]{1,0:T(8,128)(2,1)}, bf16[128,1536]{1,0:T(8,128)(2,1)}, f32[1,384]{1,0:T(1,128)}, f32[1,1536]{1,0:T(1,128)}) custom-call(bf16[128,1536]{1,0:T(8,128)(2,1)} %frames_h.1, s32[128]{0:T(128)} %mask_h.1, s32[32]{0:T(128)} %dest_h.1, s32[3,1536]{1,0:T(4,128)} %bitcast.3, s32[3,1536]{1,0:T(4,128)} %bitcast.4, f32[256,128]{1,0:T(8,128)} %cb1_h.1, ...), custom_call_target="tpu_custom_call" | custom-call | flops 8999999488 | bytes 8000000 | tf_op jit(solution)/shard_map/pallas_call | solution.py:434
  77.3 3.4 %shard_map.139 = (bf16[128,3072]{1,0:T(8,128)(2,1)}, bf16[128,1536]{1,0:T(8,128)(2,1)}, f32[384]{0:T(512)}, f32[1536]{0:T(1024)}) custom-call(bf16[128,3072]{1,0:T(8,128)(2,1)} %get-tuple-element.8.act, bf16[128,1536]{1,0:T(8,128)(2,1)} %get-tuple-element.9.mfg, f32[1,384]{1,0:T(1,128)} %get-tuple-element.10.sred, f32[1,1536]{1,0:T(1,128)} %get-tuple-element.11.gred), custom_call_target="tpu_custom_call" | custom-call | tf_op jit(solution)/shard_map/pallas_call | solution.py:465

commit v4 on v3

--- a/solution.py
+++ b/solution.py
@@ -24,9 +24,9 @@
 
 def kernel(
     frames_h, mask_h, dest_h, c1_h, c2_h, cb1_h, cb2_h, rot_h, gain_h, scale_h, cot_h,
-    act_h, mfg_h, sred, gred,
-    frames, mask, destv, c1, c2, cb1, cb2, gain, scale, cot, act, mfg,
-    outb, inb, wout, win, codef, codes, cbcat, rfull, deq, xhat, normed, ubuf, vacc, vbuf, dnorm,
+    act_h, mfg_h, sred_h, gred_h,
+    frames, mask, destv, c1, c2, cb1, cb2, gain, scale, cot, act, mfg, sred, gred,
+    outb, inb, wout, win, put, codef, codes, cbcat, rfull, deq, xhat, normed, ubuf, vacc, vbuf, dnorm,
     sbuf, sgot, smsg_b, sgot_b, smsg_c, sgot_c, ghalf, ggot_x, gmsg_z, ggot_z, gfin,
     s_in, s_out, s_frames, r_frames, s_meta, r_meta, s_own, s_c0, r_c0, s_c1, r_c1,
     s_r0, r_r0, s_r1, r_r1, s_r2, r_r2, s_rx, r_rx, s_dx, r_dx, s_red, r_red,
@@ -153,11 +153,16 @@
 
     def send_block(j, _):
         peer = (dp + j) % NDP
+        to(outb.at[block(peer), :], inb.at[block(dp), :], s_frames, r_frames, peer, fs).start()
+        return 0
+
+    def send_meta(j, _):
+        peer = (dp + j) % NDP
         to(wout.at[peer], win.at[dp], s_meta, r_meta, peer, fs).start()
-        to(outb.at[block(peer), :], inb.at[block(dp), :], s_frames, r_frames, peer, fs).start()
         return 0
 
     lax.fori_loop(1, 22, send_block, 0)
+    lax.fori_loop(1, NDP, send_meta, 0)
     own = pltpu.make_async_copy(outb.at[block(dp), :], inb.at[block(dp), :], s_own)
     own.start()
 
@@ -193,29 +198,25 @@
 
     look_up(fs, 0)
 
-    for k in (1, 3, 2):
+    def pass_codes(k):
         wait_for(code_piece(back(k), xx), r_c0.at[k - 1])
         for d in (1, 2, 3):
             peer = zlo * 16 + ((xx + d) % 4) * 4 + yy
             to(code_piece(back(k), xx), code_piece(back(k), xx), s_c1, r_c1.at[k - 1], peer, fs).start()
-    for k in (1, 3, 2):
-        wait_for(piece(back(k), xx, yy), r_r0.at[k - 1])
+
+    def pass_piece(k):
+        mine = piece(back(k), xx, yy)
+        wait_for(mine, r_r0.at[k - 1])
         for d in (1, 2, 3):
             nx = (xx + d * (1 - core)) % 4
             ny = (yy + d * core) % 4
-            to(piece(back(k), xx, yy), piece(back(k), xx, yy), s_r1, r_r1.at[k - 1], zlo * 16 + nx * 4 + ny, fs).start()
+            to(mine, mine, s_r1, r_r1.at[k - 1], zlo * 16 + nx * 4 + ny, fs).start()
         for d in (1, 2, 3):
             nx = (xx + d * core) % 4
             ny = (yy + d * (1 - core)) % 4
-            to(piece(back(k), xx, yy), piece(back(k), xx, yy), s_r2, r_r2.at[k - 1], zlo * 16 + nx * 4 + ny, fs).start()
-
-    lax.fori_loop(22, 43, send_block, 0)
-
-    for k in (1, 3):
-        wait_for(codes.at[0, 0:96, :], r_c1.at[k - 1])
-        look_up(back(k), k)
-
-    for k in (1, 3, 2):
+            to(mine, mine, s_r2, r_r2.at[k - 1], zlo * 16 + nx * 4 + ny, fs).start()
+
+    def pass_line(k):
         wait_for(rfull.at[0:144, 0:PC], r_r1.at[k - 1])
 
         def spread(n, _):
@@ -230,19 +231,23 @@
 
         lax.fori_loop(0, 9, spread, 0)
 
+    pass_piece(1)
+    pass_piece(3)
+    pass_codes(1)
+    pass_codes(3)
+    lax.fori_loop(22, 43, send_block, 0)
+    pass_piece(2)
+    pass_codes(2)
+    pass_line(1)
+    pass_line(3)
     lax.fori_loop(43, NDP, send_block, 0)
-
-    wait_for(codes.at[0, 0:96, :], r_c1.at[1])
-    look_up(back(2), 2)
-    loads[10].wait()
+    pass_line(2)
 
     for k in (1, 3, 2):
-        wait_for(rfull.at[0:576, 0:PC], r_r2.at[k - 1])
-        to(rfull.at[rows_of(back(k)), :], rfull.at[rows_of(back(k)), :], s_rx.at[k], r_rx.at[k], dp, other).start()
+        wait_for(codes.at[0, 0:96, :], r_c1.at[k - 1])
+        look_up(back(k), k)
 
     wait_for(win.at[0 : NDP - 1], r_meta)
-    wait_for(inb.at[0 : (NDP - 1) * MSG, :], r_frames)
-    own.wait()
     meta = win[...]
     mask_row = jnp.sum(meta, axis=0) - 1.0
     src_row = jnp.sum(jnp.where(meta > 0.5, iota((NDP, 1, ROWS), 0, F32), 0.0), axis=0)
@@ -251,8 +256,18 @@
     src = jnp.sum(jnp.where(eye, src_row, 0.0), axis=1, keepdims=True)
     first = src * float(MSG) + (iota((ROWS, 1), 0) % 4).astype(F32)
     for s in range(4):
-        put = jnp.where(iota((ROWS, NDP * MSG), 1, F32) == first + 4.0 * s, 1.0, 0.0).astype(BF16)
-        xhat[:, s * SEG : (s + 1) * SEG] = jnp.dot(put, inb[...], preferred_element_type=F32)
+        put[s] = jnp.where(iota((ROWS, NDP * MSG), 1, F32) == first + 4.0 * s, 1.0, 0.0).astype(BF16)
+
+    loads[10].wait()
+
+    for k in (1, 3, 2):
+        wait_for(rfull.at[0:576, 0:PC], r_r2.at[k - 1])
+        to(rfull.at[rows_of(back(k)), :], rfull.at[rows_of(back(k)), :], s_rx.at[k], r_rx.at[k], dp, other).start()
+
+    wait_for(inb.at[0 : (NDP - 1) * MSG, :], r_frames)
+    own.wait()
+    for s in range(4):
+        xhat[:, s * SEG : (s + 1) * SEG] = jnp.dot(put[s], inb[...], preferred_element_type=F32)
     xval = xhat[...]
     centered = xval - jnp.sum(xval, axis=1, keepdims=True) * (1.0 / D)
     inv = lax.rsqrt(jnp.sum(centered * centered, axis=1, keepdims=True) * (1.0 / D) + 1e-06)
@@ -394,14 +409,20 @@
 
     wait_for(sgot_c.at[0:3], r_red.at[2])
     sred[...] = jnp.sum(sgot_c[...], axis=0)
+    sred_out = pltpu.make_async_copy(sred, sred_h, s_out.at[2])
+    sred_out.start()
     wait_for(sgot_c.at[0:3], s_red.at[2])
     wait_for(gfin.at[0], r_red.at[5])
     gred[:, :HALF] = gfin[0]
     gred[:, HALF:] = gfin[1]
+    gred_out = pltpu.make_async_copy(gred, gred_h, s_out.at[3])
+    gred_out.start()
+    sred_out.wait()
+    gred_out.wait()
     wait_for(gfin.at[0], s_red.at[5])
 
 
-def finish(act, mfg, sred, gred, act_o, mfg_o, s_o, g_o, act_v, mfg_v, sems):
+def finish(act, mfg, sred, gred, act_o, mfg_o, s_o, g_o, act_v, mfg_v, s_v, g_v, s1, g1, sems):
     steps = []
     for n in range(4):
         at = pl.ds(n * 32, 32)
@@ -409,15 +430,24 @@
     for n in range(2):
         at = pl.ds(n * 64, 64)
         steps.append((mfg.at[at], mfg_v.at[at], mfg_o.at[at]))
+    steps.append((sred, s_v, None))
+    steps.append((gred, g_v, None))
     ins = [pltpu.make_async_copy(a, v, sems.at[n]) for n, (a, v, _) in enumerate(steps)]
-    outs = [pltpu.make_async_copy(v, o, sems.at[len(steps) + n]) for n, (_, v, o) in enumerate(steps)]
     for copy in ins:
         copy.start()
-    s_o[...] = sred[...].reshape(384)
-    g_o[...] = gred[...].reshape(D)
-    for arrive, leave in zip(ins, outs):
-        arrive.wait()
+    outs = []
+    for n in (6, 7, 0, 1, 2, 3, 4, 5):
+        ins[n].wait()
+        if n == 6:
+            s1[...] = s_v[...].reshape(384)
+            leave = pltpu.make_async_copy(s1, s_o, sems.at[8 + n])
+        elif n == 7:
+            g1[...] = g_v[...].reshape(D)
+            leave = pltpu.make_async_copy(g1, g_o, sems.at[8 + n])
+        else:
+            leave = pltpu.make_async_copy(steps[n][1], steps[n][2], sems.at[8 + n])
         leave.start()
+        outs.append(leave)
     for copy in outs:
         copy.wait()
 
@@ -430,18 +460,17 @@
     vm = pltpu.VMEM
     shape = jax.ShapeDtypeStruct
     hbm = pl.BlockSpec(memory_space=pltpu.HBM)
-    vmem = pl.BlockSpec(memory_space=pltpu.VMEM)
     act, mfg, sred, gred = pl.pallas_call(
         kernel,
         out_shape=(shape((ROWS, FF), BF16), shape((ROWS, D), BF16), shape((1, 384), F32), shape((1, D), F32)),
         in_specs=[hbm] * 11,
-        out_specs=(hbm, hbm, vmem, vmem),
+        out_specs=(hbm, hbm, hbm, hbm),
         scratch_shapes=[
             vm((ROWS, D), BF16), vm((ROWS,), jnp.int32), vm((32,), jnp.int32),
             vm((3, D), jnp.int32), vm((3, D), jnp.int32), vm((256, 128), F32), vm((256, 128), F32),
-            vm((D,), F32), vm((1, FF), F32), vm((ROWS, FF), BF16), vm((ROWS, FF), BF16), vm((ROWS, D), BF16),
+            vm((D,), F32), vm((1, FF), F32), vm((ROWS, FF), BF16), vm((ROWS, FF), BF16), vm((ROWS, D), BF16), vm((1, 384), F32), vm((1, D), F32),
             vm((NDP * MSG, SEG), BF16), vm((NDP * MSG, SEG), BF16),
-            vm((NDP, 1, ROWS), F32), vm((NDP, 1, ROWS), F32),
+            vm((NDP, 1, ROWS), F32), vm((NDP, 1, ROWS), F32), vm((4, ROWS, NDP * MSG), BF16),
             vm((128, 128), F32), vm((NF, 128, 128), BF16), vm((512, 256), BF16),
             vm((D, D), BF16), vm((D, FF), BF16),
             vm((ROWS, D), F32), vm((ROWS, D), BF16), vm((ROWS, D), BF16),
@@ -450,7 +479,7 @@
             vm((1, SEG), F32), vm((16, 1, SEG), F32), vm((1, SEG), F32), vm((4, 1, SEG), F32),
             vm((2, 1, HALF), F32), vm((32, 1, HALF), F32), vm((1, HALF), F32), vm((16, 1, HALF), F32),
             vm((2, 1, HALF), F32),
-            dma((11,)), dma((2,)), dma, dma, dma, dma, dma, dma((3,)), dma((3,)), dma, dma((3,)),
+            dma((11,)), dma((4,)), dma, dma, dma, dma, dma, dma((3,)), dma((3,)), dma, dma((3,)),
             dma((3,)), dma((3,)), dma, dma((3,)), dma, dma((3,)), dma((4,)), dma((4,)), dma((4,)), dma((4,)),
             dma((6,)), dma((6,)),
         ],
@@ -465,9 +494,13 @@
     return pl.pallas_call(
         finish,
         out_shape=(shape((ROWS, FF), BF16), shape((ROWS, D), BF16), shape((384,), F32), shape((D,), F32)),
-        in_specs=[hbm, hbm, vmem, vmem],
-        out_specs=(hbm, hbm, vmem, vmem),
-        scratch_shapes=[vm((ROWS, FF), BF16), vm((ROWS, D), BF16), dma((12,))],
+        in_specs=[hbm] * 4,
+        out_specs=(hbm,) * 4,
+        scratch_shapes=[
+            vm((ROWS, FF), BF16), vm((ROWS, D), BF16), vm((1, 384), F32), vm((1, D), F32), vm((384,), F32), vm((D,), F32),
+            dma((16,)),
+        ],
+        compiler_params=pltpu.CompilerParams(vmem_limit_bytes=56 * 1024 * 1024),
     )(act, mfg, sred, gred)
 
 

time: 81 us -> 82.3 us (1.016)
  Pallas kernels: 80 us -> 81.3 us
    pallas_call x1, Pallas kernels: 76.6 us -> 79 us  [body(): pl.pallas_call(kernel, out_shape=(shape((ROWS, FF), BF16), shape((ROWS, D...]
    pallas_call x1, Pallas kernels: 3.42 us -> 2.3 us  [body(): pl.pallas_call(finish, out_shape=(shape((ROWS, FF), BF16), shape((ROWS, D...]
where the time goes in v4:
time: 82.3 us; the launch traced here: 82.2 us
  Pallas kernels  81.3 us (99%)
    pallas_call x1, Pallas kernels, body(): pl.pallas_call(kernel, out_shape=(shape((ROWS, FF), BF16), shape((ROWS, D...  79 us
    pallas_call x1, Pallas kernels, body(): pl.pallas_call(finish, out_shape=(shape((ROWS, FF), BF16), shape((ROWS, D...  2.3 us

profile of v4, /device:TPU:1, one launch (start us, length us, event | category | flops | bytes accessed | tf_op | source)
XLA Modules:
  0.0 82.2 jit_solution(13433022126935075486)
XLA Ops:
  0.6 79.0 %shard_map.138 = (bf16[128,3072]{1,0:T(8,128)(2,1)}, bf16[128,1536]{1,0:T(8,128)(2,1)}, f32[1,384]{1,0:T(1,128)}, f32[1,1536]{1,0:T(1,128)}) custom-call(bf16[128,1536]{1,0:T(8,128)(2,1)} %frames_h.1, s32[128]{0:T(128)} %mask_h.1, s32[32]{0:T(128)} %dest_h.1, s32[3,1536]{1,0:T(4,128)} %bitcast.3, s32[3,1536]{1,0:T(4,128)} %bitcast.4, f32[256,128]{1,0:T(8,128)} %cb1_h.1, ...), custom_call_target="tpu_custom_call" | custom-call | flops 8999999488 | bytes 8000000 | tf_op jit(solution)/shard_map/pallas_call | solution.py:463
  79.7 2.3 %shard_map.139 = (bf16[128,3072]{1,0:T(8,128)(2,1)}, bf16[128,1536]{1,0:T(8,128)(2,1)}, f32[384]{0:T(512)}, f32[1536]{0:T(1024)}) custom-call(bf16[128,3072]{1,0:T(8,128)(2,1)} %get-tuple-element.8.act, bf16[128,1536]{1,0:T(8,128)(2,1)} %get-tuple-element.9.mfg, f32[1,384]{1,0:T(1,128)} %get-tuple-element.10.sred, f32[1,1536]{1,0:T(1,128)} %get-tuple-element.11.gred), custom_call_target="tpu_custom_call" | custom-call | tf_op jit(solution)/shard_map/pallas_call | solution.py:494

commit v5 on v4

--- a/solution.py
+++ b/solution.py
@@ -161,8 +161,8 @@
         to(wout.at[peer], win.at[dp], s_meta, r_meta, peer, fs).start()
         return 0
 
-    lax.fori_loop(1, 22, send_block, 0)
     lax.fori_loop(1, NDP, send_meta, 0)
+    lax.fori_loop(1, NDP, send_block, 0)
     own = pltpu.make_async_copy(outb.at[block(dp), :], inb.at[block(dp), :], s_own)
     own.start()
 
@@ -231,22 +231,30 @@
 
         lax.fori_loop(0, 9, spread, 0)
 
+    pass_codes(1)
+    pass_codes(3)
+    def pass_far():
+        mine = piece(back(2), xx, yy)
+        wait_for(mine, r_r0.at[1])
+
+        def direct(j, _):
+            to(mine, mine, s_r2, r_r2.at[1], zlo * 16 + (xy + j) % 16, fs).start()
+            return 0
+
+        lax.fori_loop(1, 16, direct, 0)
+
     pass_piece(1)
     pass_piece(3)
-    pass_codes(1)
-    pass_codes(3)
-    lax.fori_loop(22, 43, send_block, 0)
-    pass_piece(2)
     pass_codes(2)
+    pass_far()
+    for k in (1, 3,):
+        wait_for(codes.at[0, 0:96, :], r_c1.at[k - 1])
+        look_up(back(k), k)
     pass_line(1)
     pass_line(3)
-    lax.fori_loop(43, NDP, send_block, 0)
-    pass_line(2)
-
-    for k in (1, 3, 2):
+    for k in (2,):
         wait_for(codes.at[0, 0:96, :], r_c1.at[k - 1])
         look_up(back(k), k)
-
     wait_for(win.at[0 : NDP - 1], r_meta)
     meta = win[...]
     mask_row = jnp.sum(meta, axis=0) - 1.0
@@ -261,7 +269,8 @@
     loads[10].wait()
 
     for k in (1, 3, 2):
-        wait_for(rfull.at[0:576, 0:PC], r_r2.at[k - 1])
+        count = 720 if k == 2 else 576
+        wait_for(rfull.at[0:count, 0:PC], r_r2.at[k - 1])
         to(rfull.at[rows_of(back(k)), :], rfull.at[rows_of(back(k)), :], s_rx.at[k], r_rx.at[k], dp, other).start()
 
     wait_for(inb.at[0 : (NDP - 1) * MSG, :], r_frames)
@@ -277,15 +286,16 @@
     gain_row = gain[...].reshape(1, D)
     normed[...] = (standard * gain_row).astype(BF16)
 
-    for k in range(4):
+    for k in (0, 1, 3, 2):
         wait_for(rfull.at[rows_of(other_of(back(k))), :], r_rx.at[k])
-
-    def forward_u(n, _):
-        cols = pl.ds(pl.multiple_of(n * 512, 512), 512)
-        ubuf[:, cols] = jnp.dot(normed[...], rfull[:, cols], preferred_element_type=F32).astype(BF16)
-        return 0
-
-    lax.fori_loop(0, 3, forward_u, 0)
+        depth = pl.ds(pl.multiple_of(((zhi + 4 - k) % 4) * 384, 128), 384)
+        part = jnp.dot(normed[:, depth], rfull[depth, :], preferred_element_type=F32)
+        if k == 0:
+            vacc[...] = part
+        elif k == 2:
+            ubuf[...] = (vacc[...] + part).astype(BF16)
+        else:
+            vacc[...] += part
 
     loads[8].wait()
     loads[9].wait()
@@ -394,8 +404,8 @@
     for k in range(4):
         wait_for(rfull.at[0:192, :], s_rx.at[k])
         wait_for(deq.at[:, 0:SEG], s_dx.at[k])
-    wait_for(rfull.at[0:432, 0:PC], s_r1)
-    wait_for(rfull.at[0:432, :], s_r2)
+    wait_for(rfull.at[0:288, 0:PC], s_r1)
+    wait_for(rfull.at[0:624, 0:1152], s_r2)
     wait_for(sgot.at[0 : NF - 1], s_red.at[0])
     wait_for(sgot_b.at[0:15], s_red.at[1])
     wait_for(ggot_x.at[0:31], s_red.at[3])

time: 82.3 us -> 77.7 us (0.944)
  Pallas kernels: 81.3 us -> 76.8 us
    pallas_call x1, Pallas kernels: 79 us -> 74.5 us  [body(): pl.pallas_call(kernel, out_shape=(shape((ROWS, FF), BF16), shape((ROWS, D...]
where the time goes in v5:
time: 77.7 us; the launch traced here: 77.6 us
  Pallas kernels  76.8 us (99%)
  between operations  0.8 us (1%)
    pallas_call x1, Pallas kernels, body(): pl.pallas_call(kernel, out_shape=(shape((ROWS, FF), BF16), shape((ROWS, D...  74.5 us
    pallas_call x1, Pallas kernels, body(): pl.pallas_call(finish, out_shape=(shape((ROWS, FF), BF16), shape((ROWS, D...  2.3 us

profile of v5, /device:TPU:1, one launch (start us, length us, event | category | flops | bytes accessed | tf_op | source)
XLA Modules:
  0.0 77.6 jit_solution(3897300607821707977)
XLA Ops:
  0.6 74.5 %shard_map.138 = (bf16[128,3072]{1,0:T(8,128)(2,1)}, bf16[128,1536]{1,0:T(8,128)(2,1)}, f32[1,384]{1,0:T(1,128)}, f32[1,1536]{1,0:T(1,128)}) custom-call(bf16[128,1536]{1,0:T(8,128)(2,1)} %frames_h.1, s32[128]{0:T(128)} %mask_h.1, s32[32]{0:T(128)} %dest_h.1, s32[3,1536]{1,0:T(4,128)} %bitcast.3, s32[3,1536]{1,0:T(4,128)} %bitcast.4, f32[256,128]{1,0:T(8,128)} %cb1_h.1, ...), custom_call_target="tpu_custom_call" | custom-call | flops 8999999488 | bytes 8000000 | tf_op jit(solution)/shard_map/pallas_call | solution.py:473
  75.1 2.3 %shard_map.139 = (bf16[128,3072]{1,0:T(8,128)(2,1)}, bf16[128,1536]{1,0:T(8,128)(2,1)}, f32[384]{0:T(512)}, f32[1536]{0:T(1024)}) custom-call(bf16[128,3072]{1,0:T(8,128)(2,1)} %get-tuple-element.8.act, bf16[128,1536]{1,0:T(8,128)(2,1)} %get-tuple-element.9.mfg, f32[1,384]{1,0:T(1,128)} %get-tuple-element.10.sred, f32[1,1536]{1,0:T(1,128)} %get-tuple-element.11.gred), custom_call_target="tpu_custom_call" | custom-call | tf_op jit(solution)/shard_map/pallas_call | solution.py:504
